TPU v7x, 512 devices: a whole 4x8x8 slice. The times are simulated.
512 devices in a mesh: seq: 64 (over z, y), head: 8 (over x, core).
Axes of the slice: x: 4, y: 8, z: 8, core: 2. Of those that a mesh axis runs over, the one named last changes fastest.
Arguments:
- query_elements: bfloat16 [65536, 4096], P('seq', 'head'), may hold values from -4 to 4
- query_exponents: int32 [65536, 128], P('seq', 'head'), may hold values from -1 to 1
- key_elements: bfloat16 [65536, 512], P('seq', 'head'), may hold values from -4 to 4
- key_exponents: int32 [65536, 16], P('seq', 'head'), may hold values from -1 to 1
- value_elements: bfloat16 [65536, 512], P('seq', 'head'), may hold values from -4 to 4
- value_exponents: int32 [65536, 16], P('seq', 'head'), may hold values from -1 to 1
- query_clip_words: int32 [65536, 256], P('seq', 'head'), may hold values from 0 to 65280, as said below
- key_clip_words: int32 [65536, 32], P('seq', 'head'), may hold values from 0 to 65280, as said below
- sinks: float32 [64], P('head'), may hold values from -2 to 2
- rotation: float32 [8, 64, 64], P('head'), may hold values from -0.75 to 0.75
- output_gradient: bfloat16 [65536, 4096], P('seq', 'head'), may hold values from -120 to 120
Outputs:
- grad_q: bfloat16 [65536, 4096], P('seq', 'head')
- key_gradient_raw: bfloat16 [65536, 512], P('seq', 'head')
- value_gradient: bfloat16 [65536, 512], P('seq', 'head')
- grad_rotation: float32 [8, 64, 64], P('head')
- grad_sinks: float32 [64], P('head')
Inputs may be any that keep to these rules, and one draw needn't show every extreme that they name: `query_clip_words`: bit b of word w of a row is 1 where entry 16 w + b of the row passed the clip; a word whose upper eight bits are all set has its lower eight bits clear. `key_clip_words`: bit b of word w of a row is 1 where entry 16 w + b of the row passed the clip; a word whose upper eight bits are all set has its lower eight bits clear.
All inputs are finite; a program needn't handle non-finite values.
Results may differ from a plain program's by a relative error of at most 0.0097.
Values may be sent and summed in bfloat16 or wider, within the bound.
A program may use at most 64 MiB of HBM per device.

v0:
```python
import math

import jax
import jax.numpy as jnp
from jax import lax
from jax.sharding import PartitionSpec as P

WINDOW = 128
SHARED_EXPONENT = 32


clip_scale = 64.0
limit_factor = 0.05
negative = -1e30


def from_behind(block, axis, distance):
    devices = range(lax.axis_size(axis))
    route = [(i - distance, i) for i in devices if i - distance in devices]
    return lax.ppermute(block, axis, route)


def decode_blocks(element_vals, powers):
    row_count = element_vals.shape[0]
    scaled = (
        element_vals.astype(jnp.float32).reshape(row_count, -1, SHARED_EXPONENT)
        * jnp.exp2(powers.astype(jnp.float32))[:, :, None]
    )
    return scaled.reshape(row_count, -1).astype(jnp.bfloat16)


def unpack_words(packed):
    shifts = jnp.arange(16, dtype=jnp.int32)
    bit_vals = jnp.right_shift(packed[:, :, None], shifts[None, None, :]) & 1
    return bit_vals.reshape(packed.shape[0], -1).astype(jnp.float32)


def attend(query_blk, dout_blk, keys_blk, values, sink_logit, query_pos, key_pos):
    temper = query_blk.shape[-1] ** (-0.5)
    scores = (
        jnp.einsum("igqd,jgd->gqij", query_blk, keys_blk, preferred_element_type=jnp.float32)
        * temper
    )
    allowed = (
        (key_pos[None, :] <= query_pos[:, None])
        & (key_pos[None, :] > query_pos[:, None] - WINDOW)
        & (key_pos[None, :] >= 0)
    )
    scores = jnp.where(allowed, scores, negative)
    row_max = jnp.maximum(jnp.max(scores, axis=3), sink_logit[:, :, None])
    numerators = jnp.where(allowed, jnp.exp(scores - row_max[..., None]), 0.0)
    totals = jnp.sum(numerators, axis=3) + jnp.exp(sink_logit[:, :, None] - row_max)
    weights = numerators / totals[..., None]
    rounded = weights.astype(jnp.bfloat16)
    outputs = jnp.einsum("gqij,jgd->igqd", rounded, values, preferred_element_type=jnp.float32)
    deltas = jnp.transpose(jnp.sum(dout_blk.astype(jnp.float32) * outputs, axis=3), (1, 2, 0))
    grad_probs = jnp.einsum("igqd,jgd->gqij", dout_blk, values, preferred_element_type=jnp.float32)
    grad_scores = (weights * (grad_probs - deltas[..., None])).astype(jnp.bfloat16)
    grad_query = (
        jnp.einsum("gqij,jgd->igqd", grad_scores, keys_blk, preferred_element_type=jnp.float32)
        * temper
    )
    grad_keys = (
        jnp.einsum("gqij,igqd->jgd", grad_scores, query_blk, preferred_element_type=jnp.float32)
        * temper
    )
    grad_vals = jnp.einsum("gqij,igqd->jgd", rounded, dout_blk, preferred_element_type=jnp.float32)
    sink_terms = -jnp.sum(jnp.exp(sink_logit[:, :, None] - row_max) / totals * deltas, axis=2)
    return (grad_query, grad_keys, grad_vals, sink_terms, (row_max, totals, deltas))


def rim_terms(query_blk, dout_blk, row_max, totals, deltas, keys_blk, values):
    temper = query_blk.shape[-1] ** (-0.5)
    scores = (
        jnp.einsum("igqd,jgd->gqij", query_blk, keys_blk, preferred_element_type=jnp.float32)
        * temper
    )
    positions = jnp.arange(WINDOW, dtype=jnp.int32)
    allowed = positions[None, :] > positions[:, None]
    numerators = jnp.where(allowed, jnp.exp(scores - row_max[..., None]), 0.0)
    weights = numerators / jnp.maximum(totals, 1.0)[..., None]
    rounded = weights.astype(jnp.bfloat16)
    grad_probs = jnp.einsum("igqd,jgd->gqij", dout_blk, values, preferred_element_type=jnp.float32)
    grad_scores = (weights * (grad_probs - deltas[..., None])).astype(jnp.bfloat16)
    grad_keys = (
        jnp.einsum("gqij,igqd->jgd", grad_scores, query_blk, preferred_element_type=jnp.float32)
        * temper
    )
    grad_vals = jnp.einsum("gqij,igqd->jgd", rounded, dout_blk, preferred_element_type=jnp.float32)
    return (grad_keys, grad_vals)


def run_blocks(query_rows_list, douts, key_ext, value_ext, offset, sink_logit):
    block_count = query_rows_list.shape[0] // WINDOW

    def block(block_index):
        begin_row = block_index * WINDOW
        query_b = lax.dynamic_slice_in_dim(query_rows_list, begin_row, WINDOW, 0)
        dout_b = lax.dynamic_slice_in_dim(douts, begin_row, WINDOW, 0)
        keys_b = lax.dynamic_slice_in_dim(key_ext, begin_row, 2 * WINDOW, 0)
        values_b = lax.dynamic_slice_in_dim(value_ext, begin_row, 2 * WINDOW, 0)
        query_pos = offset + begin_row + jnp.arange(WINDOW, dtype=jnp.int32)
        key_pos = offset + begin_row - WINDOW + jnp.arange(2 * WINDOW, dtype=jnp.int32)
        return attend(query_b, dout_b, keys_b, values_b, sink_logit, query_pos, key_pos)

    return lax.map(block, jnp.arange(block_count, dtype=jnp.int32))


def per_device(
    query_elements,
    query_exponents,
    key_elements,
    key_exponents,
    value_elements,
    value_exponents,
    query_clip_words,
    key_clip_words,
    sinks,
    rotation,
    output_gradient,
):
    row_count = query_elements.shape[0]
    local_groups = rotation.shape[0]
    head_dim = rotation.shape[1]
    per_group = sinks.shape[0] // local_groups
    query_rows_list = decode_blocks(query_elements, query_exponents).reshape(
        row_count, local_groups, per_group, head_dim
    )
    key_row_list = decode_blocks(key_elements, key_exponents).reshape(
        row_count, local_groups, head_dim
    )
    value_row_list = decode_blocks(value_elements, value_exponents).reshape(
        row_count, local_groups, head_dim
    )
    output_grad_list = output_gradient.reshape(row_count, local_groups, per_group, head_dim)
    sink_row_list = sinks.reshape(local_groups, per_group)
    offset = lax.axis_index("seq") * row_count
    all_tokens = row_count * lax.axis_size("seq")
    all_heads = sinks.shape[0] * lax.axis_size("head")
    limit_value = limit_factor * math.sqrt(all_tokens * all_heads * head_dim)
    prev_keys, prev_vals = from_behind(
        (key_row_list[row_count - WINDOW :], value_row_list[row_count - WINDOW :]), "seq", 1
    )
    results = run_blocks(
        query_rows_list,
        output_grad_list,
        jnp.concatenate([prev_keys, key_row_list], 0),
        jnp.concatenate([prev_vals, value_row_list], 0),
        offset,
        sink_row_list,
    )
    grad_query, grad_keys, grad_vals, sink_terms, row_stats = results
    next_query, next_dout = from_behind(
        (query_rows_list[:WINDOW], output_grad_list[:WINDOW]), "seq", -1
    )
    next_max, next_total, next_delta = from_behind(
        (row_stats[0][0], row_stats[1][0], row_stats[2][0]), "seq", -1
    )
    back_keys, back_vals = rim_terms(
        next_query,
        next_dout,
        next_max,
        next_total,
        next_delta,
        key_row_list[row_count - WINDOW :],
        value_row_list[row_count - WINDOW :],
    )
    key_total = grad_keys[:, WINDOW:] + jnp.concatenate(
        [grad_keys[1:, :WINDOW], back_keys[None]], 0
    )
    value_total = grad_vals[:, WINDOW:] + jnp.concatenate(
        [grad_vals[1:, :WINDOW], back_vals[None]], 0
    )
    key_total = key_total.reshape(row_count, local_groups, head_dim)
    value_gradient = value_total.reshape(row_count, local_groups * head_dim).astype(jnp.bfloat16)
    grad_query = grad_query.reshape(row_count, local_groups, per_group, head_dim)
    query_flags = unpack_words(query_clip_words).reshape(
        row_count, local_groups, per_group, head_dim
    )
    key_flags = unpack_words(key_clip_words).reshape(row_count, local_groups, head_dim)
    masked_query = (grad_query * query_flags).astype(jnp.bfloat16)
    masked_keys = (key_total * key_flags).astype(jnp.bfloat16)
    rotation_low = rotation.astype(jnp.bfloat16)
    grad_q = jnp.einsum(
        "tgqd,ged->tgqe", masked_query, rotation_low, preferred_element_type=jnp.float32
    )
    grad_q = grad_q.astype(jnp.bfloat16).reshape(row_count, -1)
    key_gradient_raw = jnp.einsum(
        "tgd,ged->tge", masked_keys, rotation_low, preferred_element_type=jnp.float32
    )
    key_gradient_raw = key_gradient_raw.astype(jnp.bfloat16).reshape(row_count, -1)
    partial_value = jnp.einsum(
        "tgqd,tgqe->gde", query_rows_list, masked_query, preferred_element_type=jnp.float32
    )
    partial_value = partial_value + jnp.einsum(
        "tgd,tge->gde", key_row_list, masked_keys, preferred_element_type=jnp.float32
    )
    sink_part = jnp.sum(sink_terms, axis=0).reshape(-1)
    summed, sink_sum = lax.psum((partial_value, sink_part), "seq")
    raw_grad = jnp.einsum("gde,gef->gdf", rotation, summed, precision=lax.Precision.HIGHEST)
    squares = lax.psum(jnp.sum(raw_grad * raw_grad), "head")
    grad_rotation = raw_grad * (clip_scale / jnp.maximum(jnp.sqrt(squares), limit_value))
    return (grad_q, key_gradient_raw, value_gradient, grad_rotation, sink_sum)


def solution(mesh):
    return jax.shard_map(
        per_device,
        mesh=mesh,
        in_specs=(
            P("seq", "head"),
            P("seq", "head"),
            P("seq", "head"),
            P("seq", "head"),
            P("seq", "head"),
            P("seq", "head"),
            P("seq", "head"),
            P("seq", "head"),
            P("head"),
            P("head", None, None),
            P("seq", "head"),
        ),
        out_specs=(
            P("seq", "head"),
            P("seq", "head"),
            P("seq", "head"),
            P("head", None, None),
            P("head"),
        ),
        check_vma=False,
    )
```

profile of v0, /device:TPU:1, one launch (start us, length us, event | category | flops | bytes accessed | tf_op | source)
XLA Modules:
  0.0 508.0 jit_solution(15169535315948217598)
XLA Ops:
  2.9 4.6 collective-permute-start
  9.8 3.3 collective-permute-start.1
  26.7 145.5 %while.25 = (s32[]{:T(128)}, f32[8,128,1,8,64]{1,0,4,3,2:T(8,128)}, f32[8,256,1,64]{1,0,3,2:T(8,128)}, f32[8,256,1,64]{1,3,2,0:T(8,128)}, f32[8,1,8]{2,1,0:T(1,1...) while((s32[]{:T(128)}, f32[8,128,1,8,64]{1,0,4,3,2:T(8,128)}, ...), condition=%wide.region_5.6_spmd, body=%wide.region_0.5_spmd.sunk | while | flops 206990464 | bytes 9088008 | solution.py:106
  31.7 7.7 %dynamic_update_slice.66 = f32[8,128,1,8,64]{1,0,4,3,2:T(8,128)} dynamic-update-slice(f32[8,128,1,8,64]{1,0,4,3,2:T(8,128)} %get-tuple-element.411, f32[1,128,1,8,64]{1,0,4,3,2:T(1,128)S(1)} %bitcast.371, s32[]{:T(128)} %get-tuple-element.410, s32[]{:T(128)} %constant.100.clone.1..sunk, s32[]{:T(128)} %constant.100.clone.1..sunk, s32[]{:T(128)} %constant.100.clone.1..sunk, s32[]{:T(128)} %constant.100.clone.1..sunk) | dynamic-update-slice | bytes 524292 | tf_op jit(solution)/shard_map/while/body/jit(dynamic_update_index_in_dim)/dynamic_update_slice | solution.py:106
  42.5 2.4 dynamic_update_slice.67
  49.9 7.7 %dynamic_update_slice.66 = f32[8,128,1,8,64]{1,0,4,3,2:T(8,128)} dynamic-update-slice(f32[8,128,1,8,64]{1,0,4,3,2:T(8,128)} %get-tuple-element.411, f32[1,128,1,8,64]{1,0,4,3,2:T(1,128)S(1)} %bitcast.371, s32[]{:T(128)} %get-tuple-element.410, s32[]{:T(128)} %constant.100.clone.1..sunk, s32[]{:T(128)} %constant.100.clone.1..sunk, s32[]{:T(128)} %constant.100.clone.1..sunk, s32[]{:T(128)} %constant.100.clone.1..sunk) | dynamic-update-slice | bytes 524292 | tf_op jit(solution)/shard_map/while/body/jit(dynamic_update_index_in_dim)/dynamic_update_slice | solution.py:106
  60.7 2.4 dynamic_update_slice.67
  68.1 7.7 %dynamic_update_slice.66 = f32[8,128,1,8,64]{1,0,4,3,2:T(8,128)} dynamic-update-slice(f32[8,128,1,8,64]{1,0,4,3,2:T(8,128)} %get-tuple-element.411, f32[1,128,1,8,64]{1,0,4,3,2:T(1,128)S(1)} %bitcast.371, s32[]{:T(128)} %get-tuple-element.410, s32[]{:T(128)} %constant.100.clone.1..sunk, s32[]{:T(128)} %constant.100.clone.1..sunk, s32[]{:T(128)} %constant.100.clone.1..sunk, s32[]{:T(128)} %constant.100.clone.1..sunk) | dynamic-update-slice | bytes 524292 | tf_op jit(solution)/shard_map/while/body/jit(dynamic_update_index_in_dim)/dynamic_update_slice | solution.py:106
  78.9 2.4 dynamic_update_slice.67
  86.2 7.7 %dynamic_update_slice.66 = f32[8,128,1,8,64]{1,0,4,3,2:T(8,128)} dynamic-update-slice(f32[8,128,1,8,64]{1,0,4,3,2:T(8,128)} %get-tuple-element.411, f32[1,128,1,8,64]{1,0,4,3,2:T(1,128)S(1)} %bitcast.371, s32[]{:T(128)} %get-tuple-element.410, s32[]{:T(128)} %constant.100.clone.1..sunk, s32[]{:T(128)} %constant.100.clone.1..sunk, s32[]{:T(128)} %constant.100.clone.1..sunk, s32[]{:T(128)} %constant.100.clone.1..sunk) | dynamic-update-slice | bytes 524292 | tf_op jit(solution)/shard_map/while/body/jit(dynamic_update_index_in_dim)/dynamic_update_slice | solution.py:106
  97.1 2.4 dynamic_update_slice.67
  104.4 7.7 %dynamic_update_slice.66 = f32[8,128,1,8,64]{1,0,4,3,2:T(8,128)} dynamic-update-slice(f32[8,128,1,8,64]{1,0,4,3,2:T(8,128)} %get-tuple-element.411, f32[1,128,1,8,64]{1,0,4,3,2:T(1,128)S(1)} %bitcast.371, s32[]{:T(128)} %get-tuple-element.410, s32[]{:T(128)} %constant.100.clone.1..sunk, s32[]{:T(128)} %constant.100.clone.1..sunk, s32[]{:T(128)} %constant.100.clone.1..sunk, s32[]{:T(128)} %constant.100.clone.1..sunk) | dynamic-update-slice | bytes 524292 | tf_op jit(solution)/shard_map/while/body/jit(dynamic_update_index_in_dim)/dynamic_update_slice | solution.py:106
  115.3 2.4 dynamic_update_slice.67
  122.6 7.7 %dynamic_update_slice.66 = f32[8,128,1,8,64]{1,0,4,3,2:T(8,128)} dynamic-update-slice(f32[8,128,1,8,64]{1,0,4,3,2:T(8,128)} %get-tuple-element.411, f32[1,128,1,8,64]{1,0,4,3,2:T(1,128)S(1)} %bitcast.371, s32[]{:T(128)} %get-tuple-element.410, s32[]{:T(128)} %constant.100.clone.1..sunk, s32[]{:T(128)} %constant.100.clone.1..sunk, s32[]{:T(128)} %constant.100.clone.1..sunk, s32[]{:T(128)} %constant.100.clone.1..sunk) | dynamic-update-slice | bytes 524292 | tf_op jit(solution)/shard_map/while/body/jit(dynamic_update_index_in_dim)/dynamic_update_slice | solution.py:106
  133.5 2.4 dynamic_update_slice.67
  140.8 7.7 %dynamic_update_slice.66 = f32[8,128,1,8,64]{1,0,4,3,2:T(8,128)} dynamic-update-slice(f32[8,128,1,8,64]{1,0,4,3,2:T(8,128)} %get-tuple-element.411, f32[1,128,1,8,64]{1,0,4,3,2:T(1,128)S(1)} %bitcast.371, s32[]{:T(128)} %get-tuple-element.410, s32[]{:T(128)} %constant.100.clone.1..sunk, s32[]{:T(128)} %constant.100.clone.1..sunk, s32[]{:T(128)} %constant.100.clone.1..sunk, s32[]{:T(128)} %constant.100.clone.1..sunk) | dynamic-update-slice | bytes 524292 | tf_op jit(solution)/shard_map/while/body/jit(dynamic_update_index_in_dim)/dynamic_update_slice | solution.py:106
  151.6 2.4 dynamic_update_slice.67
  159.0 7.7 %dynamic_update_slice.66 = f32[8,128,1,8,64]{1,0,4,3,2:T(8,128)} dynamic-update-slice(f32[8,128,1,8,64]{1,0,4,3,2:T(8,128)} %get-tuple-element.411, f32[1,128,1,8,64]{1,0,4,3,2:T(1,128)S(1)} %bitcast.371, s32[]{:T(128)} %get-tuple-element.410, s32[]{:T(128)} %constant.100.clone.1..sunk, s32[]{:T(128)} %constant.100.clone.1..sunk, s32[]{:T(128)} %constant.100.clone.1..sunk, s32[]{:T(128)} %constant.100.clone.1..sunk) | dynamic-update-slice | bytes 524292 | tf_op jit(solution)/shard_map/while/body/jit(dynamic_update_index_in_dim)/dynamic_update_slice | solution.py:106
  169.8 2.4 dynamic_update_slice.67
  178.1 2.9 reshape.570
  181.0 2.7 multiply_convert_fusion
  183.7 2.5 convert_element_type.145
  195.6 238.2 %all-reduce = (f32[64,64]{1,0:T(8,128)S(1)}, f32[8]{0:T(128)}) all-reduce(f32[64,64]{1,0:T(8,128)S(1)} %convolution_add_fusion, f32[8]{0:T(128)S(1)} %reduce_sum.52), channel_id=1, replica_groups=mesh['seq'=64,'head'=8] {'seq'}, use_global_device_ids=true, to_apply=%region_6.7 | all-reduce | flops 4104 | bytes 32832 | tf_op jit(solution)/shard_map/psum | solution.py:199
  434.7 69.9 %psum.22 = f32[]{:T(128)} all-reduce(f32[]{:T(128)} %get-tuple-element.286), channel_id=1, replica_groups=mesh['seq'=64,'head'=8] {'head'}, use_global_device_ids=true, to_apply=%region_8.9 | all-reduce | flops 1 | bytes 8 | tf_op jit(solution)/shard_map/psum | solution.py:201
  (248 shorter events, 95.4 us)
Async XLA Ops:
  0.6 14.0 %copy-start.11 = (s32[1024,16]{0,1:T(8,128)S(1)}, s32[1024,16]{0,1:T(8,128)}, u32[]{:S(2)}) copy-start(s32[1024,16]{0,1:T(8,128)} %param.14) | copy-start | bytes 196612
  2.9 22.3 %collective-permute-start = (bf16[128,1,64]{0,2,1:T(8,128)(2,1)}, bf16[128,1,64]{0,2,1:T(8,128)(2,1)}, u32[]{:S(2)}, u32[]{:S(2)}) collective-permute-start(bf16[128,1,64]{0,2,1:T(8,128)(2,1)} %slice_bitcast_fusion.1), channel_id=1, source_target_pairs={{0,8},{8,16},{16,24},{24,32},{32,40},{40,48},{48,56},{56,64},{64,7... | collective-permute-start | bytes 49160 | tf_op jit(solution)/shard_map/ppermute | solution.py:20
  9.8 7.1 %slice-start = ((bf16[1024,512]{1,0:T(8,128)(2,1)}), bf16[128,512]{1,0:T(8,128)(2,1)S(1)}, s32[]{:S(2)}) async-start(bf16[1024,512]{1,0:T(8,128)(2,1)} %param.23), calls=%async_computation | async-start | bytes 262144 | tf_op jit(solution)/shard_map/slice | solution.py:154
  9.8 9.8 %copy-start.4 = (bf16[1024,512]{1,0:T(8,128)(2,1)S(1)}, bf16[1024,512]{1,0:T(8,128)(2,1)}, u32[]{:S(2)}) copy-start(bf16[1024,512]{1,0:T(8,128)(2,1)} %param.23) | copy-start | bytes 3145732
  9.8 16.2 %collective-permute-start.1 = (bf16[128,1,64]{0,2,1:T(8,128)(2,1)}, bf16[128,1,64]{0,2,1:T(8,128)(2,1)}, u32[]{:S(2)}, u32[]{:S(2)}) collective-permute-start(bf16[128,1,64]{0,2,1:T(8,128)(2,1)} %slice_bitcast_fusion), channel_id=1, source_target_pairs={{0,8},{8,16},{16,24},{24,32},{32,40},{40,48},{48,56},{56,64},{64,7... | collective-permute-start | bytes 49160 | tf_op jit(solution)/shard_map/ppermute | solution.py:20
  14.7 6.3 %copy-start.12 = (s32[1024,4]{0,1:T(4,128)S(1)}, s32[1024,4]{0,1:T(4,128)}, u32[]{:S(2)}) copy-start(s32[1024,4]{0,1:T(4,128)} %param.20) | copy-start | bytes 49156
  15.0 6.9 %copy-start.10 = (s32[1024,32]{0,1:T(8,128)S(1)}, s32[1024,32]{0,1:T(8,128)}, u32[]{:S(2)}) copy-start(s32[1024,32]{0,1:T(8,128)} %param.19) | copy-start | bytes 393220
  15.7 176.0 %collective-permute-start.2 = (bf16[128,1,8,64]{0,3,2,1:T(8,128)(2,1)}, bf16[128,1,8,64]{0,3,2,1:T(8,128)(2,1)}, u32[]{:S(2)}, u32[]{:S(2)}) collective-permute-start(bf16[128,1,8,64]{0,3,2,1:T(8,128)(2,1)} %bitcast.51), channel_id=1, source_target_pairs={{8,0},{16,8},{24,16},{32,24},{40,32},{48,40},{56,48},{64,56},{72,6... | collective-permute-start | bytes 393224 | tf_op jit(solution)/shard_map/ppermute | solution.py:20
  17.7 175.2 %collective-permute-start.5 = (bf16[128,1,8,64]{0,3,2,1:T(8,128)(2,1)}, bf16[128,1,8,64]{0,3,2,1:T(8,128)(2,1)}, u32[]{:S(2)}, u32[]{:S(2)}) collective-permute-start(bf16[128,1,8,64]{0,3,2,1:T(8,128)(2,1)} %bitcast.61), channel_id=1, source_target_pairs={{8,0},{16,8},{24,16},{32,24},{40,32},{48,40},{56,48},{64,56},{72,6... | collective-permute-start | bytes 393224 | tf_op jit(solution)/shard_map/ppermute | solution.py:20
  22.1 1.3 copy-start
  23.5 3.3 copy-start.9
  172.9 18.8 %collective-permute-start.4 = (f32[1,8,128]{2,1,0:T(8,128)S(1)}, f32[1,8,128]{2,1,0:T(8,128)S(1)}, u32[]{:S(2)}, u32[]{:S(2)}) collective-permute-start(f32[1,8,128]{2,1,0:T(8,128)S(1)} %slice_bitcast_fusion.3), channel_id=1, source_target_pairs={{8,0},{16,8},{24,16},{32,24},{40,32},{48,40},{56,48},{64,56},{72,6... | collective-permute-start | bytes 12296 | tf_op jit(solution)/shard_map/ppermute | solution.py:20
  174.9 16.8 %collective-permute-start.3 = (f32[1,8,128]{2,1,0:T(8,128)S(1)}, f32[1,8,128]{2,1,0:T(8,128)S(1)}, u32[]{:S(2)}, u32[]{:S(2)}) collective-permute-start(f32[1,8,128]{2,1,0:T(8,128)S(1)} %slice_bitcast_fusion.4), channel_id=1, source_target_pairs={{8,0},{16,8},{24,16},{32,24},{40,32},{48,40},{56,48},{64,56},{72,6... | collective-permute-start | bytes 12296 | tf_op jit(solution)/shard_map/ppermute | solution.py:20
  176.8 16.1 %collective-permute-start.6 = (f32[1,8,128]{2,1,0:T(8,128)S(1)}, f32[1,8,128]{2,1,0:T(8,128)S(1)}, u32[]{:S(2)}, u32[]{:S(2)}) collective-permute-start(f32[1,8,128]{2,1,0:T(8,128)S(1)} %slice_bitcast_fusion.2), channel_id=1, source_target_pairs={{8,0},{16,8},{24,16},{32,24},{40,32},{48,40},{56,48},{64,56},{72,6... | collective-permute-start | bytes 12296 | tf_op jit(solution)/shard_map/ppermute | solution.py:20
  178.1 2.9 copy-start.2
  183.7 2.5 copy-start.1
  186.2 2.1 copy-start.3
  186.2 2.1 copy-start.8
  188.3 1.0 copy-start.6
  188.7 3.0 copy-start.13
  191.6 2.8 copy-start.5
  192.9 314.2 %copy-start.7 = (f32[8,256,1,64]{1,3,2,0:T(8,128)S(1)}, f32[8,256,1,64]{1,3,2,0:T(8,128)}, u32[]{:S(2)}) copy-start(f32[8,256,1,64]{1,3,2,0:T(8,128)} %get-tuple-element.237) | copy-start | bytes 1572868
where the time goes:
time: 511 us; the launch traced here: 508 us
  blocking collectives  308 us (60%)
  local copies, waits for them, and re-layouts  107 us (21%)
  matrix products  49 us (10%)
  other arithmetic  21.7 us (4%)
  starting transfers between devices  14.3 us (3%)
  loops' own time  5.8 us (1%)
    psum x1, blocking collectives, per_device(): summed, sink_sum = lax.psum((partial_value, sink_part), 'seq')  238 us
    dynamic_update_slice x24, local copies, waits for them, and re-layouts, run_blocks(): return lax.map(block, jnp.arange(block_count, dtype=jnp.int32))  81.4 us
    psum x1, blocking collectives, per_device(): squares = lax.psum(jnp.sum(raw_grad * raw_grad), 'head')  69.9 us
    dot_general x8, matrix products, attend(): jnp.einsum('gqij,igqd->jgd', rounded, dout_blk, preferred_element_type=jn...  15.1 us
    ppermute x7, starting transfers between devices, from_behind(): return lax.ppermute(block, axis, route)  14.3 us
    dot_general x8, matrix products, attend(): jnp.einsum('igqd,jgd->gqij', dout_blk, values, preferred_element_type=jnp...  10.6 us
  transfers between devices with their start and end apart: 7, of which 0 were waited for; matrix products, arithmetic and copies ran while one was open for 33% of the time, Pallas kernels for 0%

commit v1 on v0

v1 whole, which is shorter than its diff:
```python
import functools
import math

import jax
import jax.numpy as jnp
from jax import lax
from jax.experimental import pallas as pl
from jax.experimental.pallas import tpu as pltpu
from jax.sharding import PartitionSpec as P

WINDOW = 128
HEAD = 64
PAIR = 2 * HEAD
clip_scale = 64.0
limit_factor = 0.05
temper = 0.125
negative = -1e30
f32 = jnp.float32
bf16 = jnp.bfloat16
MESH = pl.DeviceIdType.MESH

NN = (((1,), (0,)), ((), ()))
NT = (((1,), (1,)), ((), ()))


def mm(a, b, dims=NN):
    return lax.dot_general(a, b, dims, preferred_element_type=f32)


def spread(ref, first, count, times, cols):
    width = WINDOW
    return jnp.concatenate(
        [jnp.broadcast_to(ref[first + r : first + r + 1, cols], (times, width)) for r in range(count)], axis=0
    )


def kernel(sizes, limit_value, *refs):
    (
        qe_hbm, qx_hbm, kt_hbm, kx_hbm, vt_hbm, vx_hbm, qc_hbm, kc_hbm, sinks, rot_hbm, do_hbm,
        gq_hbm, gk_hbm, gv_hbm, gr_hbm, gs_hbm,
        q_s, d_s, g_s, qx_s, kt_s, kx_s, vt_s, vx_s, qc_s, kc_s, rot_s,
        scale_s, kv_t, k_row, v_row, dkv, rb_s, part_s, sinkacc, tri_s, back_in, gk_s, gv_s,
        buf_a1, buf_b1, buf_a2, buf_b2, sq_buf, gr_s, gs_s,
        q_sem, d_sem, g_sem, in_sem, out_sem, halo_sem, back_sem,
        a1_send, a1_recv, b1_send, b1_recv, a2_send, a2_recv, b2_send, b2_recv, h_send, h_recv,
    ) = refs
    nz, ny, nh, blocks, heads = sizes
    ns = nz * ny
    pairs = heads // 2
    me_s = lax.axis_index("seq")
    me_h = lax.axis_index("head")
    me_z, me_y = me_s // ny, lax.rem(me_s, ny)
    nxt, prv = lax.rem(me_s + 1, ns), lax.rem(me_s + ns - 1, ns)

    def seq_dev(s):
        return (s, me_h)

    z_peers = [(lax.rem(me_z + k, nz)) for k in range(1, nz)]
    y_peers = [(lax.rem(me_y + k, ny)) for k in range(1, ny)]
    h_peers = [(lax.rem(me_h + k, nh)) for k in range(1, nh)]

    barrier = pltpu.get_barrier_semaphore()
    targets = [(nxt, me_h), (prv, me_h)]
    targets += [(z * ny + me_y, me_h) for z in z_peers]
    targets += [(me_z * ny + y, me_h) for y in y_peers]
    targets += [(me_s, h) for h in h_peers]
    for dev in targets:
        pl.semaphore_signal(barrier, inc=1, device_id=dev, device_id_type=MESH)

    small = [
        (kt_hbm, kt_s), (kx_hbm, kx_s), (vt_hbm, vt_s), (vx_hbm, vx_s),
        (qx_hbm, qx_s), (qc_hbm, qc_s), (kc_hbm, kc_s), (rot_hbm, rot_s),
    ]
    small_copies = [pltpu.make_async_copy(a, b, in_sem.at[n]) for n, (a, b) in enumerate(small)]
    for c in small_copies[:4]:
        c.start()

    def q_copy(b):
        rows = pl.ds(pl.multiple_of(b * WINDOW, WINDOW), WINDOW)
        return pltpu.make_async_copy(qe_hbm.at[rows], q_s.at[rows], q_sem.at[b])

    def d_copy(b):
        rows = pl.ds(pl.multiple_of(b * WINDOW, WINDOW), WINDOW)
        return pltpu.make_async_copy(do_hbm.at[rows], d_s.at[rows], d_sem.at[b])

    def g_copy(b):
        rows = pl.ds(pl.multiple_of(b * WINDOW, WINDOW), WINDOW)
        return pltpu.make_async_copy(g_s.at[rows], gq_hbm.at[rows], g_sem.at[b])

    def at_step(n):
        return jnp.where(n < 5, n + 1, jnp.where(n == 5, 0, n))

    for n in range(blocks):
        b = [1, 2, 3, 4, 5, 0, 6, 7][n]
        q_copy(b).start()
        d_copy(b).start()
        if n == 0:
            for c in small_copies[4:]:
                c.start()

    p_iota = lax.broadcasted_iota(jnp.int32, (WINDOW, 2 * WINDOW), 0)
    i_iota = lax.rem(lax.broadcasted_iota(jnp.int32, (WINDOW, 2 * WINDOW), 1), WINDOW)
    tri_s[...] = jnp.where(p_iota <= i_iota, 1.0, 0.0).astype(bf16)
    part_s[...] = jnp.zeros_like(part_s)
    sinkacc[...] = jnp.zeros_like(sinkacc)
    dkv[...] = jnp.zeros_like(dkv)

    for c in small_copies[:4]:
        c.wait()
    ksc = jnp.exp2(kx_s[...].astype(f32)) * temper
    vsc = jnp.exp2(vx_s[...].astype(f32))
    for half in range(2):
        rr = slice(32 * half, 32 * half + 32)
        k8 = (kt_s[rr, :].astype(f32) * ksc[half : half + 1, :]).astype(bf16)
        vv = (vt_s[rr, :].astype(f32) * vsc[half : half + 1, :]).astype(bf16)
        kv_t[32 * half : 32 * half + 32, WINDOW:] = k8
        kv_t[HEAD + 32 * half : HEAD + 32 * half + 32, WINDOW:] = vv

    def rows_of(cb):
        at = pl.ds(pl.multiple_of(cb * WINDOW, WINDOW), WINDOW)
        both = kv_t[:, at]
        k_row[at, :] = both[:HEAD].T
        v_row[at, :] = both[HEAD:].T

    def rows_step(cb, carry):
        rows_of(cb)
        return carry

    lax.fori_loop(1, blocks + 1, rows_step, 0)

    for c in small_copies[4:]:
        c.wait()
    scale_s[...] = jnp.exp2(qx_s[...].astype(f32))
    rlow = rot_s[...].astype(bf16)
    rlow_t = rot_s[...].T.astype(bf16)
    zero = jnp.zeros((HEAD, HEAD), bf16)
    rb_s[...] = jnp.concatenate(
        [jnp.concatenate([rlow_t, zero], axis=1), jnp.concatenate([zero, rlow_t], axis=1)], axis=0
    )

    halo = pltpu.make_async_remote_copy(
        src_ref=kv_t.at[:, pl.ds(blocks * WINDOW, WINDOW)],
        dst_ref=kv_t.at[:, pl.ds(0, WINDOW)],
        send_sem=halo_sem.at[0], recv_sem=halo_sem.at[1],
        device_id=(nxt, me_h), device_id_type=MESH,
    )
    back = pltpu.make_async_remote_copy(
        src_ref=dkv.at[:, pl.ds(0, WINDOW)],
        dst_ref=back_in,
        send_sem=back_sem.at[0], recv_sem=back_sem.at[1],
        device_id=(prv, me_h), device_id_type=MESH,
    )
    bits = jnp.left_shift(1, lax.broadcasted_iota(jnp.int32, (16, WINDOW), 0))
    bits64 = jnp.concatenate([bits] * 4, axis=0)

    def step(n, carry):
        b = at_step(n)

        @pl.when(n == 3)
        def _():
            pl.semaphore_wait(barrier, len(targets))
            halo.start()

        @pl.when(n == 5)
        def _():
            halo.wait()
            rows_of(0)

        q_copy(b).wait()
        d_copy(b).wait()
        cols = pl.ds(pl.multiple_of(b * WINDOW, WINDOW), WINDOW)
        wide = pl.ds(pl.multiple_of(b * WINDOW, WINDOW), 2 * WINDOW)
        hidden = jnp.where((b == 0) & (me_s == 0), negative, 0.0)
        k2 = k_row[wide, :]
        v2 = v_row[wide, :]
        k2t = kv_t[:HEAD, wide]
        dk = jnp.zeros((HEAD, 2 * WINDOW), f32)
        dv = jnp.zeros((HEAD, 2 * WINDOW), f32)
        part = jnp.zeros((HEAD, HEAD), f32)
        tri = p_iota <= i_iota
        for pr in range(pairs):
            lanes = slice(pr * PAIR, (pr + 1) * PAIR)
            qt = q_s[cols, lanes].T * spread(scale_s, 4 * pr, 4, 32, cols).astype(bf16)
            dt = d_s[cols, lanes].T
            q2 = jnp.concatenate([qt[:HEAD], qt[HEAD:]], axis=1)
            d2 = jnp.concatenate([dt[:HEAD], dt[HEAD:]], axis=1)
            s_all = mm(k2, q2)
            s = jnp.where(tri, s_all[WINDOW:], s_all[:WINDOW] + hidden)
            sink = jnp.concatenate(
                [jnp.full((1, WINDOW), sinks[2 * pr + h], f32) for h in range(2)], axis=1
            )
            top = jnp.maximum(jnp.max(s, axis=0, keepdims=True), sink)
            e = jnp.exp(s - top)
            es = jnp.exp(sink - top)
            inv = 1.0 / (jnp.sum(e, axis=0, keepdims=True) + es)
            w = e * inv
            dp_all = mm(v2, d2)
            dp = jnp.where(tri, dp_all[WINDOW:], dp_all[:WINDOW])
            t = w * dp
            delta = jnp.sum(t, axis=0, keepdims=True)
            ds = t - w * delta
            sk = es * inv * delta
            sinkacc[2 * pr : 2 * pr + 1, :] -= sk[:, :WINDOW]
            sinkacc[2 * pr + 1 : 2 * pr + 2, :] -= sk[:, WINDOW:]
            wb = w.astype(bf16)
            sb = ds.astype(bf16)
            trib = tri_s[...]
            w_cur = wb * trib
            s_cur = sb * trib
            w2 = jnp.concatenate([wb - w_cur, w_cur], axis=0)
            s2 = jnp.concatenate([sb - s_cur, s_cur], axis=0)
            dv = dv + mm(d2, w2, NT)
            dk = dk + mm(q2, s2, NT)
            gqt = mm(k2t, s2)
            m2 = []
            for h in range(2):
                words = spread(qc_s, 4 * (2 * pr + h), 4, 16, cols)
                keep = jnp.bitwise_and(words, bits64) != 0
                m2.append(jnp.where(keep, gqt[:, h * WINDOW : (h + 1) * WINDOW], 0.0).astype(bf16))
            part = part + mm(q2, jnp.concatenate(m2, axis=1), NT)
            rows_q = jnp.concatenate(m2, axis=0).T
            g_s[cols, lanes] = mm(rows_q, rb_s[...]).astype(bf16)
        dkv[:HEAD, wide] += dk
        dkv[HEAD:, wide] += dv
        part_s[...] += part
        g_copy(b).start()

        @pl.when(n == 5)
        def _():
            back.start()

        return carry

    lax.fori_loop(0, blocks, step, 0)
    back.wait()

    last = pl.ds(blocks * WINDOW, WINDOW)
    dkv[:, last] += back_in[...]

    def key_step(cb, carry):
        at = pl.ds(pl.multiple_of(cb * WINDOW, WINDOW), WINDOW)
        ext = pl.ds(pl.multiple_of((cb + 1) * WINDOW, WINDOW), WINDOW)
        keep = jnp.bitwise_and(spread(kc_s, 0, 4, 16, at), bits64) != 0
        mk = jnp.where(keep, dkv[:HEAD, ext] * temper, 0.0).astype(bf16)
        gk_s[:, at] = mm(rlow, mk).astype(bf16)
        gv_s[:, at] = dkv[HEAD:, ext].astype(bf16)
        part_s[...] += mm(kv_t[:HEAD, ext], mk, NT) * (1.0 / temper)
        return carry

    lax.fori_loop(0, blocks, key_step, 0)
    gk_copy = pltpu.make_async_copy(gk_s, gk_hbm, out_sem.at[0])
    gv_copy = pltpu.make_async_copy(gv_s, gv_hbm, out_sem.at[1])
    gk_copy.start()
    gv_copy.start()

    cut = buf_a1.shape[1]
    part = part_s[...]
    folded = jnp.concatenate([part[: HEAD // 2], part[HEAD // 2 :]], axis=1)
    buf_a1[pl.ds(me_z, 1)] = folded[:cut][None]
    buf_b1[pl.ds(me_y, 1)] = jnp.concatenate([folded[cut:], sinkacc[...]], axis=0)[None]

    def exchange(buf, me, peers, device, send, recv):
        copies = []
        for k, peer in enumerate(peers):
            copies.append(
                pltpu.make_async_remote_copy(
                    src_ref=buf.at[me], dst_ref=buf.at[me],
                    send_sem=send.at[k], recv_sem=recv.at[k],
                    device_id=device(peer), device_id_type=MESH,
                )
            )
        for c in copies:
            c.start()
        return copies

    def along_z(z):
        return (z * ny + me_y, me_h)

    def along_y(y):
        return (me_z * ny + y, me_h)

    def along_h(h):
        return (me_s, h)

    def total(buf, count):
        acc = buf[0]
        for k in range(1, count):
            acc = acc + buf[k]
        return acc

    copies_a = exchange(buf_a1, me_z, z_peers, along_z, a1_send, a1_recv)
    copies_b = exchange(buf_b1, me_y, y_peers, along_y, b1_send, b1_recv)
    for c in copies_a:
        c.wait()
    buf_a2[pl.ds(me_y, 1)] = total(buf_a1, nz)[None]
    copies_a = exchange(buf_a2, me_y, y_peers, along_y, a2_send, a2_recv)
    for c in copies_b:
        c.wait()
    buf_b2[pl.ds(me_z, 1)] = total(buf_b1, ny)[None]
    copies_b = exchange(buf_b2, me_z, z_peers, along_z, b2_send, b2_recv)
    for c in copies_a:
        c.wait()
    for c in copies_b:
        c.wait()
    tot_a = total(buf_a2, ny)
    tot_b = total(buf_b2, nz)
    rows_b = HEAD // 2 - cut
    whole = jnp.concatenate([tot_a, tot_b[:rows_b]], axis=0)
    summed = jnp.concatenate([whole[:, :HEAD], whole[:, HEAD:]], axis=0)
    raw = lax.dot_general(
        rot_s[...], summed, NN, precision=lax.Precision.HIGHEST, preferred_element_type=f32
    )
    sq = jnp.sum(jnp.sum(raw * raw, axis=0, keepdims=True), axis=1, keepdims=True)
    sq_buf[pl.ds(me_h, 1)] = jnp.broadcast_to(sq, (8, 128))[None]
    copies_h = exchange(sq_buf, me_h, h_peers, along_h, h_send, h_recv)
    gs_s[...] = jnp.sum(tot_b[rows_b:].T, axis=0, keepdims=True)
    gs_copy = pltpu.make_async_copy(gs_s, gs_hbm, out_sem.at[2])
    gs_copy.start()
    for c in copies_h:
        c.wait()
    norm = jnp.sqrt(total(sq_buf, nh)[:1, :HEAD])
    gr_s[...] = raw * (clip_scale / jnp.maximum(norm, limit_value))
    gr_copy = pltpu.make_async_copy(gr_s, gr_hbm, out_sem.at[3])
    gr_copy.start()

    def g_wait(b, carry):
        g_copy(b).wait()
        return carry

    lax.fori_loop(0, blocks, g_wait, 0)
    gk_copy.wait()
    gv_copy.wait()
    gs_copy.wait()
    gr_copy.wait()


def per_device(split, ns, nh, qe, qx, ke, kx, ve, vx, qc, kc, sinks, rot, dout):
    tokens, width = qe.shape
    heads = width // HEAD
    blocks = tokens // WINDOW
    nz, ny = split
    limit_value = limit_factor * math.sqrt(tokens * ns * heads * nh * HEAD)
    cut = 16
    rest = HEAD // 2 - cut + 8
    any_space = pl.BlockSpec(memory_space=pl.ANY)
    vmem = pltpu.VMEM
    dma = pltpu.SemaphoreType.DMA
    ext = tokens + WINDOW
    outs = pl.pallas_call(
        functools.partial(kernel, (nz, ny, nh, blocks, heads), limit_value),
        out_shape=(
            jax.ShapeDtypeStruct((tokens, width), bf16),
            jax.ShapeDtypeStruct((HEAD, tokens), bf16),
            jax.ShapeDtypeStruct((HEAD, tokens), bf16),
            jax.ShapeDtypeStruct((HEAD, HEAD), f32),
            jax.ShapeDtypeStruct((1, heads), f32),
        ),
        in_specs=[any_space] * 8 + [pl.BlockSpec(memory_space=pltpu.SMEM)] + [any_space] * 2,
        out_specs=(any_space,) * 5,
        scratch_shapes=[
            vmem((tokens, width), bf16),
            vmem((tokens, width), bf16),
            vmem((tokens, width), bf16),
            vmem((2 * heads, tokens), jnp.int32),
            vmem((HEAD, tokens), bf16),
            vmem((2, tokens), jnp.int32),
            vmem((HEAD, tokens), bf16),
            vmem((2, tokens), jnp.int32),
            vmem((4 * heads, tokens), jnp.int32),
            vmem((4, tokens), jnp.int32),
            vmem((HEAD, HEAD), f32),
            vmem((2 * heads, tokens), f32),
            vmem((2 * HEAD, ext), bf16),
            vmem((ext, HEAD), bf16),
            vmem((ext, HEAD), bf16),
            vmem((2 * HEAD, ext), f32),
            vmem((PAIR, PAIR), bf16),
            vmem((HEAD, HEAD), f32),
            vmem((heads, WINDOW), f32),
            vmem((WINDOW, 2 * WINDOW), bf16),
            vmem((2 * HEAD, WINDOW), f32),
            vmem((HEAD, tokens), bf16),
            vmem((HEAD, tokens), bf16),
            vmem((nz, cut, 128), f32),
            vmem((ny, rest, 128), f32),
            vmem((ny, cut, 128), f32),
            vmem((nz, rest, 128), f32),
            vmem((nh, 8, 128), f32),
            vmem((HEAD, HEAD), f32),
            vmem((1, heads), f32),
            dma((blocks,)),
            dma((blocks,)),
            dma((blocks,)),
            dma((8,)),
            dma((4,)),
            dma((2,)),
            dma((2,)),
            dma((nz,)), dma((nz,)), dma((ny,)), dma((ny,)),
            dma((ny,)), dma((ny,)), dma((nz,)), dma((nz,)),
            dma((nh,)), dma((nh,)),
        ],
        compiler_params=pltpu.CompilerParams(
            collective_id=0, has_side_effects=True, vmem_limit_bytes=63 * 1024 * 1024
        ),
    )(qe, qx.T, ke.T, kx.T, ve.T, vx.T, qc.T, kc.T, sinks, rot.reshape(HEAD, HEAD), dout)
    gq, gk, gv, gr, gs = outs
    return (gq, gk.T, gv.T, gr[None], gs.reshape(heads))


def solution(mesh):
    ns, nh = mesh.shape["seq"], mesh.shape["head"]
    ny = 1 << ((ns.bit_length() - 1) // 2)
    seq_head = P("seq", "head")
    return jax.shard_map(
        functools.partial(per_device, (ns // ny, ny), ns, nh),
        mesh=mesh,
        in_specs=(seq_head,) * 8 + (P("head"), P("head", None, None), seq_head),
        out_specs=(seq_head, seq_head, seq_head, P("head", None, None), P("head")),
        check_vma=False,
    )
```

time: 511 us -> 57.1 us (0.11)
  blocking collectives: 308 us -> 0 us
  local copies, waits for them, and re-layouts: 107 us -> 5.18 us
  Pallas kernels: 0 us -> 50.9 us
  matrix products: 49 us -> 0 us
  other arithmetic: 21.7 us -> 0 us
  starting transfers between devices: 14.3 us -> 0 us
  loops' own time: 5.8 us -> 0 us
    psum x2 -> x0, blocking collectives: 308 us -> none  [the longest x1 238 us: per_device(): summed, sink_sum = lax.psum((partial_value, sink_part), 'seq')]
    dynamic_update_slice x24 -> x0, local copies, waits for them, and re-layouts: 81.4 us -> none  [run_blocks(): return lax.map(block, jnp.arange(block_count, dtype=jnp.int32))]
    pallas_call x0 -> x1, Pallas kernels: none -> 50.9 us  [per_device(): pl.pallas_call(functools.partial(kernel, (nz, ny, nh, blocks, heads), lim...]
    dot_general x56 -> x0, matrix products: 49 us -> none  [the longest x8 15.1 us: attend(): jnp.einsum('gqij,igqd->jgd', rounded, dout_blk, preferred_element_type=jn...]
    ppermute x7 -> x0, starting transfers between devices: 14.3 us -> none  [from_behind(): return lax.ppermute(block, axis, route)]
    convert_element_type x7 -> x0, other arithmetic: 7.07 us -> none  [the longest x2 4.77 us: per_device(): masked_query = (grad_query * query_flags).astype(jnp.bfloat16)]
    another operation x1 -> x0, loops' own time: 5.8 us -> none  [run_blocks(): return lax.map(block, jnp.arange(block_count, dtype=jnp.int32))]
    dynamic_update_slice x16 -> x0, other arithmetic: 5.49 us -> none  [run_blocks(): return lax.map(block, jnp.arange(block_count, dtype=jnp.int32))]
  transfers between devices with their start and end apart: 7 -> 0, of which waited for: 0 -> 0; matrix products, arithmetic and copies ran while one was open for 33% -> 0% of each run, Pallas kernels for 0% -> 0%
where the time goes in v1:
time: 57.1 us; the launch traced here: 56.8 us
  Pallas kernels  50.9 us (89%)
  local copies, waits for them, and re-layouts  5.18 us (9%)
  between operations  0.66 us (1%)
    pallas_call x1, Pallas kernels, per_device(): pl.pallas_call(functools.partial(kernel, (nz, ny, nh, blocks, heads), lim...  50.9 us
    unnamed x13, local copies, waits for them, and re-layouts  5.18 us

profile of v1, /device:TPU:1, one launch (start us, length us, event | category | flops | bytes accessed | tf_op | source)
XLA Modules:
  0.0 56.8 jit_solution(12099649510378831587)
XLA Ops:
  0.6 50.9 %shard_map.146 = (bf16[1024,512]{1,0:T(8,128)(2,1)}, bf16[64,1024]{1,0:T(8,128)(2,1)}, bf16[64,1024]{1,0:T(8,128)(2,1)}, f32[64,64]{1,0:T(8,128)}, f32[1,8]{1,0:T(1,128)}) custom-call(bf16[1024,512]{1,0:T(8,128)(2,1)} %refs_0_.1, s32[16,1024]{1,0:T(8,128)} %bitcast.17, bf16[64,1024]{1,0:T(8,128)(2,1)} %bitcast.12, s32[2,1024]{1,0:T(2,128)} %bitcast.21, ...), custom_call_target="tpu_custom_call" | custom-call | tf_op jit(solution)/shard_map/pallas_call | solution.py:349
  51.6 0.0 copy-start.1
  51.6 2.3 %copy.21 = bf16[1024,512]{1,0:T(8,128)(2,1)} copy(bf16[1024,512]{1,0:T(8,128)(2,1)} %get-tuple-element.20) | data formatting | bytes 2097152
  53.9 0.0 copy-done.1
  53.9 0.0 copy-start
  53.9 0.7 %copy.22 = bf16[1024,64]{0,1:T(8,128)(2,1)} copy(bf16[1024,64]{0,1:T(8,128)(2,1)S(1)} %bitcast.16) | data formatting | bytes 262144
  54.6 0.3 copy-done
  54.8 0.0 copy-start.2
  54.9 0.7 %copy.23 = bf16[1024,64]{0,1:T(8,128)(2,1)} copy(bf16[1024,64]{0,1:T(8,128)(2,1)S(1)} %bitcast.15) | data formatting | bytes 262144
  55.5 0.1 copy-done.2
  55.6 0.0 copy-start.3
  55.6 0.6 %copy.24 = f32[1,64,64]{2,1,0:T(8,128)} copy(f32[1,64,64]{2,1,0:T(8,128)S(1)} %bitcast.19) | data formatting | bytes 32768
  56.2 0.0 copy-done.3
  56.3 0.5 copy.25
Async XLA Ops:
  51.6 2.3 %copy-start.1 = (bf16[64,1024]{1,0:T(8,128)(2,1)S(1)}, bf16[64,1024]{1,0:T(8,128)(2,1)}, u32[]{:S(2)}) copy-start(bf16[64,1024]{1,0:T(8,128)(2,1)} %get-tuple-element.11) | copy-start | bytes 393220
  53.9 1.0 %copy-start = (bf16[64,1024]{1,0:T(8,128)(2,1)S(1)}, bf16[64,1024]{1,0:T(8,128)(2,1)}, u32[]{:S(2)}) copy-start(bf16[64,1024]{1,0:T(8,128)(2,1)} %get-tuple-element.12) | copy-start | bytes 393220
  54.8 0.8 %copy-start.2 = (f32[64,64]{1,0:T(8,128)S(1)}, f32[64,64]{1,0:T(8,128)}, u32[]{:S(2)}) copy-start(f32[64,64]{1,0:T(8,128)} %get-tuple-element.13) | copy-start | bytes 49156
  55.6 0.7 %copy-start.3 = (f32[1,8]{1,0:T(1,128)S(1)}, f32[1,8]{1,0:T(1,128)}, u32[]{:S(2)}) copy-start(f32[1,8]{1,0:T(1,128)} %get-tuple-element.14) | copy-start | bytes 100

commit v2 on v1

--- a/solution.py
+++ b/solution.py
@@ -9,6 +9,8 @@
 from jax.sharding import PartitionSpec as P
 
 WINDOW = 128
+LAGS = (4, 8, 12)
+SHARES = 4
 HEAD = 64
 PAIR = 2 * HEAD
 clip_scale = 64.0
@@ -38,9 +40,9 @@
     (
         qe_hbm, qx_hbm, kt_hbm, kx_hbm, vt_hbm, vx_hbm, qc_hbm, kc_hbm, sinks, rot_hbm, do_hbm,
         gq_hbm, gk_hbm, gv_hbm, gr_hbm, gs_hbm,
-        q_s, d_s, g_s, qx_s, kt_s, kx_s, vt_s, vx_s, qc_s, kc_s, rot_s,
-        scale_s, kv_t, k_row, v_row, dkv, rb_s, part_s, sinkacc, tri_s, back_in, gk_s, gv_s,
-        buf_a1, buf_b1, buf_a2, buf_b2, sq_buf, gr_s, gs_s,
+        q_s, d_s, mq_s, qx_s, kt_s, kx_s, vt_s, vx_s, qc_s, kc_s, rot_s,
+        scale_s, kv_t, k_row, v_row, dk_s, dv_s, d2_s, w_s, rb_s, part_s, sinkacc, tri_s, back_in, back_in_v, g_s, gk_s, gv_s, gr_s, gs_s,
+        buf_a1, buf_b1, buf_a2, buf_b2, sq_buf,
         q_sem, d_sem, g_sem, in_sem, out_sem, halo_sem, back_sem,
         a1_send, a1_recv, b1_send, b1_recv, a2_send, a2_recv, b2_send, b2_recv, h_send, h_recv,
     ) = refs
@@ -87,11 +89,8 @@
         rows = pl.ds(pl.multiple_of(b * WINDOW, WINDOW), WINDOW)
         return pltpu.make_async_copy(g_s.at[rows], gq_hbm.at[rows], g_sem.at[b])
 
-    def at_step(n):
-        return jnp.where(n < 5, n + 1, jnp.where(n == 5, 0, n))
-
     for n in range(blocks):
-        b = [1, 2, 3, 4, 5, 0, 6, 7][n]
+        b = [1, 2, 3, 4, 0, 5, 6, 7][n]
         q_copy(b).start()
         d_copy(b).start()
         if n == 0:
@@ -103,7 +102,8 @@
     tri_s[...] = jnp.where(p_iota <= i_iota, 1.0, 0.0).astype(bf16)
     part_s[...] = jnp.zeros_like(part_s)
     sinkacc[...] = jnp.zeros_like(sinkacc)
-    dkv[...] = jnp.zeros_like(dkv)
+    dk_s[...] = jnp.zeros_like(dk_s)
+    dv_s[...] = jnp.zeros_like(dv_s)
 
     for c in small_copies[:4]:
         c.wait()
@@ -145,119 +145,143 @@
         device_id=(nxt, me_h), device_id_type=MESH,
     )
     back = pltpu.make_async_remote_copy(
-        src_ref=dkv.at[:, pl.ds(0, WINDOW)],
+        src_ref=dk_s.at[:, pl.ds(0, WINDOW)],
         dst_ref=back_in,
         send_sem=back_sem.at[0], recv_sem=back_sem.at[1],
         device_id=(prv, me_h), device_id_type=MESH,
     )
+    back_v = pltpu.make_async_remote_copy(
+        src_ref=dv_s.at[:, pl.ds(0, WINDOW)],
+        dst_ref=back_in_v,
+        send_sem=back_sem.at[2], recv_sem=back_sem.at[3],
+        device_id=(prv, me_h), device_id_type=MESH,
+    )
     bits = jnp.left_shift(1, lax.broadcasted_iota(jnp.int32, (16, WINDOW), 0))
     bits64 = jnp.concatenate([bits] * 4, axis=0)
 
+    sink_rows = [
+        jnp.concatenate([jnp.full((1, WINDOW), sinks[2 * pr + h], f32) for h in range(2)], axis=1)
+        for pr in range(pairs)
+    ]
+
     def step(n, carry):
-        b = at_step(n)
-
-        @pl.when(n == 3)
+        @pl.when(n == 1)
         def _():
             pl.semaphore_wait(barrier, len(targets))
             halo.start()
 
-        @pl.when(n == 5)
+        @pl.when(n == 2)
         def _():
             halo.wait()
             rows_of(0)
 
-        q_copy(b).wait()
-        d_copy(b).wait()
-        cols = pl.ds(pl.multiple_of(b * WINDOW, WINDOW), WINDOW)
-        wide = pl.ds(pl.multiple_of(b * WINDOW, WINDOW), 2 * WINDOW)
-        hidden = jnp.where((b == 0) & (me_s == 0), negative, 0.0)
-        k2 = k_row[wide, :]
-        v2 = v_row[wide, :]
-        k2t = kv_t[:HEAD, wide]
-        dk = jnp.zeros((HEAD, 2 * WINDOW), f32)
-        dv = jnp.zeros((HEAD, 2 * WINDOW), f32)
-        part = jnp.zeros((HEAD, HEAD), f32)
+        both = [2 * n + 1 - jnp.where(n == 2, 5, 0) + jnp.where(n == 3, -1, 0), 2 * n + 2 - jnp.where(n >= 2, 1, 0)]
+        views = []
+        for b in both:
+            q_copy(b).wait()
+            d_copy(b).wait()
+            cols = pl.ds(pl.multiple_of(b * WINDOW, WINDOW), WINDOW)
+            wide = pl.ds(pl.multiple_of(b * WINDOW, WINDOW), 2 * WINDOW)
+            views.append((b, cols, wide))
+        hidden = jnp.where((both[0] == 0) & (me_s == 0), negative, 0.0)
         tri = p_iota <= i_iota
-        for pr in range(pairs):
+        trib = tri_s[...]
+        units = [(k, pr) for k in range(2) for pr in range(pairs)]
+        hold = {}
+
+        def stage_a(k, pr):
+            b, cols, wide = views[k]
             lanes = slice(pr * PAIR, (pr + 1) * PAIR)
             qt = q_s[cols, lanes].T * spread(scale_s, 4 * pr, 4, 32, cols).astype(bf16)
             dt = d_s[cols, lanes].T
             q2 = jnp.concatenate([qt[:HEAD], qt[HEAD:]], axis=1)
             d2 = jnp.concatenate([dt[:HEAD], dt[HEAD:]], axis=1)
-            s_all = mm(k2, q2)
-            s = jnp.where(tri, s_all[WINDOW:], s_all[:WINDOW] + hidden)
-            sink = jnp.concatenate(
-                [jnp.full((1, WINDOW), sinks[2 * pr + h], f32) for h in range(2)], axis=1
-            )
+            d2_s[b, :, 2 * pr * WINDOW : 2 * (pr + 1) * WINDOW] = d2
+            s_all = mm(k_row[wide, :], q2)
+            before = s_all[:WINDOW] + hidden if k == 0 else s_all[:WINDOW]
+            s = jnp.where(tri, s_all[WINDOW:], before)
+            dp_all = mm(v_row[wide, :], d2)
+            dp = jnp.where(tri, dp_all[WINDOW:], dp_all[:WINDOW])
+            hold[k, pr] = (q2, s, dp)
+
+        def stage_b(k, pr):
+            b, cols, wide = views[k]
+            q2, s, dp = hold[k, pr]
+            sink = sink_rows[pr]
             top = jnp.maximum(jnp.max(s, axis=0, keepdims=True), sink)
             e = jnp.exp(s - top)
             es = jnp.exp(sink - top)
             inv = 1.0 / (jnp.sum(e, axis=0, keepdims=True) + es)
             w = e * inv
-            dp_all = mm(v2, d2)
-            dp = jnp.where(tri, dp_all[WINDOW:], dp_all[:WINDOW])
             t = w * dp
             delta = jnp.sum(t, axis=0, keepdims=True)
             ds = t - w * delta
             sk = es * inv * delta
             sinkacc[2 * pr : 2 * pr + 1, :] -= sk[:, :WINDOW]
             sinkacc[2 * pr + 1 : 2 * pr + 2, :] -= sk[:, WINDOW:]
-            wb = w.astype(bf16)
+            w_s[b, :, 2 * pr * WINDOW : 2 * (pr + 1) * WINDOW] = w.astype(bf16)
             sb = ds.astype(bf16)
-            trib = tri_s[...]
-            w_cur = wb * trib
             s_cur = sb * trib
-            w2 = jnp.concatenate([wb - w_cur, w_cur], axis=0)
-            s2 = jnp.concatenate([sb - s_cur, s_cur], axis=0)
-            dv = dv + mm(d2, w2, NT)
-            dk = dk + mm(q2, s2, NT)
-            gqt = mm(k2t, s2)
+            hold[k, pr] = (q2, jnp.concatenate([sb - s_cur, s_cur], axis=0))
+
+        def stage_c(k, pr):
+            b, cols, wide = views[k]
+            q2, s2 = hold[k, pr]
+            gqt = mm(kv_t[:HEAD, wide], s2)
+            dk = mm(q2, s2, NT)
+            dks[k] = dk if dks[k] is None else dks[k] + dk
+            hold[k, pr] = (q2, gqt)
+
+        def stage_d(k, pr):
+            b, cols, wide = views[k]
+            lanes = slice(pr * PAIR, (pr + 1) * PAIR)
+            q2, gqt = hold.pop((k, pr))
             m2 = []
             for h in range(2):
                 words = spread(qc_s, 4 * (2 * pr + h), 4, 16, cols)
                 keep = jnp.bitwise_and(words, bits64) != 0
                 m2.append(jnp.where(keep, gqt[:, h * WINDOW : (h + 1) * WINDOW], 0.0).astype(bf16))
-            part = part + mm(q2, jnp.concatenate(m2, axis=1), NT)
-            rows_q = jnp.concatenate(m2, axis=0).T
-            g_s[cols, lanes] = mm(rows_q, rb_s[...]).astype(bf16)
-        dkv[:HEAD, wide] += dk
-        dkv[HEAD:, wide] += dv
-        part_s[...] += part
-        g_copy(b).start()
-
-        @pl.when(n == 5)
+            mq_s[lanes, cols] = jnp.concatenate(m2, axis=0)
+            part = mm(q2, jnp.concatenate(m2, axis=1), NT)
+            parts[0] = part if parts[0] is None else parts[0] + part
+
+        dks = [None, None]
+        parts = [None]
+        for t in range(len(units) + LAGS[2]):
+            for lag, stage in zip((0,) + LAGS, (stage_a, stage_b, stage_c, stage_d)):
+                if 0 <= t - lag < len(units):
+                    stage(*units[t - lag])
+        for (b, cols, wide), dk in zip(views, dks):
+            dk_s[:, wide] += dk
+        part_s[...] += parts[0]
+
+        @pl.when(n == 2)
         def _():
             back.start()
 
         return carry
 
-    lax.fori_loop(0, blocks, step, 0)
+    lax.fori_loop(0, blocks // 2, step, 0)
     back.wait()
 
     last = pl.ds(blocks * WINDOW, WINDOW)
-    dkv[:, last] += back_in[...]
-
-    def key_step(cb, carry):
-        at = pl.ds(pl.multiple_of(cb * WINDOW, WINDOW), WINDOW)
-        ext = pl.ds(pl.multiple_of((cb + 1) * WINDOW, WINDOW), WINDOW)
-        keep = jnp.bitwise_and(spread(kc_s, 0, 4, 16, at), bits64) != 0
-        mk = jnp.where(keep, dkv[:HEAD, ext] * temper, 0.0).astype(bf16)
-        gk_s[:, at] = mm(rlow, mk).astype(bf16)
-        gv_s[:, at] = dkv[HEAD:, ext].astype(bf16)
-        part_s[...] += mm(kv_t[:HEAD, ext], mk, NT) * (1.0 / temper)
-        return carry
-
-    lax.fori_loop(0, blocks, key_step, 0)
-    gk_copy = pltpu.make_async_copy(gk_s, gk_hbm, out_sem.at[0])
-    gv_copy = pltpu.make_async_copy(gv_s, gv_hbm, out_sem.at[1])
-    gk_copy.start()
-    gv_copy.start()
+    dk_s[:, last] += back_in[...]
+
+    keep = jnp.bitwise_and(
+        jnp.concatenate([jnp.broadcast_to(kc_s[r : r + 1, :], (16, blocks * WINDOW)) for r in range(4)], axis=0),
+        jnp.left_shift(1, lax.rem(lax.broadcasted_iota(jnp.int32, (HEAD, blocks * WINDOW), 0), 16)),
+    ) != 0
+    mk = jnp.where(keep, dk_s[:, WINDOW:] * temper, 0.0).astype(bf16)
+    gk_s[...] = mk
+    part_s[...] += mm(kv_t[:HEAD, WINDOW:], mk, NT) * (1.0 / temper)
 
     cut = buf_a1.shape[1]
     part = part_s[...]
     folded = jnp.concatenate([part[: HEAD // 2], part[HEAD // 2 :]], axis=1)
-    buf_a1[pl.ds(me_z, 1)] = folded[:cut][None]
-    buf_b1[pl.ds(me_y, 1)] = jnp.concatenate([folded[cut:], sinkacc[...]], axis=0)[None]
+    buf_a1[pl.ds(me_z, 1)] = folded[:cut].astype(bf16)[None]
+    buf_b1[pl.ds(me_y, 1)] = (
+        jnp.concatenate([folded[cut:], sinkacc[...], jnp.zeros_like(sinkacc)], axis=0).astype(bf16)[None]
+    )
 
     def exchange(buf, me, peers, device, send, recv):
         copies = []
@@ -283,21 +307,41 @@
         return (me_s, h)
 
     def total(buf, count):
-        acc = buf[0]
+        acc = buf[0].astype(f32)
         for k in range(1, count):
-            acc = acc + buf[k]
+            acc = acc + buf[k].astype(f32)
         return acc
 
     copies_a = exchange(buf_a1, me_z, z_peers, along_z, a1_send, a1_recv)
     copies_b = exchange(buf_b1, me_y, y_peers, along_y, b1_send, b1_recv)
+
+    def turn(b, carry):
+        cols = pl.ds(pl.multiple_of(b * WINDOW, WINDOW), WINDOW)
+        for pr in range(pairs):
+            lanes = slice(pr * PAIR, (pr + 1) * PAIR)
+            g_s[cols, lanes] = mm(mq_s[lanes, cols].T, rb_s[...]).astype(bf16)
+        g_copy(b).start()
+        return carry
+
+    def values(b, carry):
+        wide = pl.ds(pl.multiple_of(b * WINDOW, WINDOW), 2 * WINDOW)
+        wb = w_s[b]
+        w_cur = wb * jnp.concatenate([tri_s[...]] * pairs, axis=1)
+        dv_s[:, wide] += mm(d2_s[b], jnp.concatenate([wb - w_cur, w_cur], axis=0), NT)
+        return carry
+
+    values(0, 0)
+    back_v.start()
+    lax.fori_loop(1, blocks, values, 0)
     for c in copies_a:
         c.wait()
-    buf_a2[pl.ds(me_y, 1)] = total(buf_a1, nz)[None]
+    buf_a2[pl.ds(me_y, 1)] = total(buf_a1, nz).astype(bf16)[None]
     copies_a = exchange(buf_a2, me_y, y_peers, along_y, a2_send, a2_recv)
     for c in copies_b:
         c.wait()
-    buf_b2[pl.ds(me_z, 1)] = total(buf_b1, ny)[None]
+    buf_b2[pl.ds(me_z, 1)] = total(buf_b1, ny).astype(bf16)[None]
     copies_b = exchange(buf_b2, me_z, z_peers, along_z, b2_send, b2_recv)
+    lax.fori_loop(0, blocks, turn, 0)
     for c in copies_a:
         c.wait()
     for c in copies_b:
@@ -313,25 +357,57 @@
     sq = jnp.sum(jnp.sum(raw * raw, axis=0, keepdims=True), axis=1, keepdims=True)
     sq_buf[pl.ds(me_h, 1)] = jnp.broadcast_to(sq, (8, 128))[None]
     copies_h = exchange(sq_buf, me_h, h_peers, along_h, h_send, h_recv)
-    gs_s[...] = jnp.sum(tot_b[rows_b:].T, axis=0, keepdims=True)
-    gs_copy = pltpu.make_async_copy(gs_s, gs_hbm, out_sem.at[2])
-    gs_copy.start()
+    gs_s[...] = jnp.sum(tot_b[rows_b : rows_b + heads].T, axis=0, keepdims=True)
+    gk_s[...] = mm(rlow, gk_s[...]).astype(bf16)
+    back_v.wait()
+    dv_s[:, last] += back_in_v[...]
+    gv_s[...] = dv_s[:, WINDOW:].astype(bf16)
+    outs = [
+        pltpu.make_async_copy(a, b, out_sem.at[n])
+        for n, (a, b) in enumerate([(gk_s, gk_hbm), (gv_s, gv_hbm), (gs_s, gs_hbm), (gr_s, gr_hbm)])
+    ]
+    for c in outs[:3]:
+        c.start()
     for c in copies_h:
         c.wait()
     norm = jnp.sqrt(total(sq_buf, nh)[:1, :HEAD])
     gr_s[...] = raw * (clip_scale / jnp.maximum(norm, limit_value))
-    gr_copy = pltpu.make_async_copy(gr_s, gr_hbm, out_sem.at[3])
-    gr_copy.start()
+    outs[3].start()
 
     def g_wait(b, carry):
         g_copy(b).wait()
         return carry
 
     lax.fori_loop(0, blocks, g_wait, 0)
-    gk_copy.wait()
-    gv_copy.wait()
-    gs_copy.wait()
-    gr_copy.wait()
+    for c in outs:
+        c.wait()
+
+
+def store(*refs):
+    srcs, dsts, held, in_sems, out_sems = refs[:5], refs[5:10], refs[10:15], refs[15], refs[16]
+    parts = [(n, None) for n in (4, 3)]
+    share = srcs[0].shape[0] // SHARES
+    parts += [(0, pl.ds(n * share, share)) for n in range(SHARES)]
+    parts += [(n, None) for n in (1, 2)]
+
+    def view(ref, rows):
+        return ref if rows is None else ref.at[rows]
+
+    loads = [
+        pltpu.make_async_copy(view(srcs[n], rows), view(held[n], rows), in_sems.at[k])
+        for k, (n, rows) in enumerate(parts)
+    ]
+    stores = [
+        pltpu.make_async_copy(view(held[n], rows), view(dsts[n], rows), out_sems.at[k])
+        for k, (n, rows) in enumerate(parts)
+    ]
+    for c in loads:
+        c.start()
+    for c, d in zip(loads, stores):
+        c.wait()
+        d.start()
+    for d in stores:
+        d.wait()
 
 
 def per_device(split, ns, nh, qe, qx, ke, kx, ve, vx, qc, kc, sinks, rot, dout):
@@ -341,26 +417,27 @@
     nz, ny = split
     limit_value = limit_factor * math.sqrt(tokens * ns * heads * nh * HEAD)
     cut = 16
-    rest = HEAD // 2 - cut + 8
+    rest = HEAD // 2 - cut + 16
     any_space = pl.BlockSpec(memory_space=pl.ANY)
     vmem = pltpu.VMEM
     dma = pltpu.SemaphoreType.DMA
     ext = tokens + WINDOW
+    shapes = (
+        jax.ShapeDtypeStruct((tokens, width), bf16),
+        jax.ShapeDtypeStruct((HEAD, tokens), bf16),
+        jax.ShapeDtypeStruct((HEAD, tokens), bf16),
+        jax.ShapeDtypeStruct((HEAD, HEAD), f32),
+        jax.ShapeDtypeStruct((1, heads), f32),
+    )
     outs = pl.pallas_call(
         functools.partial(kernel, (nz, ny, nh, blocks, heads), limit_value),
-        out_shape=(
-            jax.ShapeDtypeStruct((tokens, width), bf16),
-            jax.ShapeDtypeStruct((HEAD, tokens), bf16),
-            jax.ShapeDtypeStruct((HEAD, tokens), bf16),
-            jax.ShapeDtypeStruct((HEAD, HEAD), f32),
-            jax.ShapeDtypeStruct((1, heads), f32),
-        ),
+        out_shape=shapes,
         in_specs=[any_space] * 8 + [pl.BlockSpec(memory_space=pltpu.SMEM)] + [any_space] * 2,
         out_specs=(any_space,) * 5,
         scratch_shapes=[
             vmem((tokens, width), bf16),
             vmem((tokens, width), bf16),
-            vmem((tokens, width), bf16),
+            vmem((width, tokens), bf16),
             vmem((2 * heads, tokens), jnp.int32),
             vmem((HEAD, tokens), bf16),
             vmem((2, tokens), jnp.int32),
@@ -373,37 +450,48 @@
             vmem((2 * HEAD, ext), bf16),
             vmem((ext, HEAD), bf16),
             vmem((ext, HEAD), bf16),
-            vmem((2 * HEAD, ext), f32),
+            vmem((HEAD, ext), f32),
+            vmem((HEAD, ext), f32),
+            vmem((blocks, HEAD, heads * WINDOW), bf16),
+            vmem((blocks, WINDOW, heads * WINDOW), bf16),
             vmem((PAIR, PAIR), bf16),
             vmem((HEAD, HEAD), f32),
             vmem((heads, WINDOW), f32),
             vmem((WINDOW, 2 * WINDOW), bf16),
-            vmem((2 * HEAD, WINDOW), f32),
+            vmem((HEAD, WINDOW), f32),
+            vmem((HEAD, WINDOW), f32),
+            vmem((tokens, width), bf16),
             vmem((HEAD, tokens), bf16),
             vmem((HEAD, tokens), bf16),
-            vmem((nz, cut, 128), f32),
-            vmem((ny, rest, 128), f32),
-            vmem((ny, cut, 128), f32),
-            vmem((nz, rest, 128), f32),
-            vmem((nh, 8, 128), f32),
             vmem((HEAD, HEAD), f32),
             vmem((1, heads), f32),
+            vmem((nz, cut, 128), bf16),
+            vmem((ny, rest, 128), bf16),
+            vmem((ny, cut, 128), bf16),
+            vmem((nz, rest, 128), bf16),
+            vmem((nh, 8, 128), f32),
             dma((blocks,)),
             dma((blocks,)),
             dma((blocks,)),
             dma((8,)),
             dma((4,)),
             dma((2,)),
-            dma((2,)),
+            dma((4,)),
             dma((nz,)), dma((nz,)), dma((ny,)), dma((ny,)),
             dma((ny,)), dma((ny,)), dma((nz,)), dma((nz,)),
             dma((nh,)), dma((nh,)),
         ],
         compiler_params=pltpu.CompilerParams(
-            collective_id=0, has_side_effects=True, vmem_limit_bytes=63 * 1024 * 1024
+            collective_id=0, has_side_effects=True, vmem_limit_bytes=61 * 1024 * 1024
         ),
     )(qe, qx.T, ke.T, kx.T, ve.T, vx.T, qc.T, kc.T, sinks, rot.reshape(HEAD, HEAD), dout)
-    gq, gk, gv, gr, gs = outs
+    gq, gk, gv, gr, gs = pl.pallas_call(
+        store,
+        out_shape=shapes,
+        in_specs=[any_space] * 5,
+        out_specs=(any_space,) * 5,
+        scratch_shapes=[vmem(x.shape, x.dtype) for x in shapes] + [dma((SHARES + 4,))] * 2,
+    )(*outs)
     return (gq, gk.T, gv.T, gr[None], gs.reshape(heads))
 
 

time: 57.1 us -> 43.4 us (0.76)
  Pallas kernels: 50.9 us -> 42.6 us
  local copies, waits for them, and re-layouts: 5.18 us -> 0 us
    pallas_call x1, Pallas kernels: 50.9 us -> 40.4 us  [per_device(): pl.pallas_call(functools.partial(kernel, (nz, ny, nh, blocks, heads), lim...]
    unnamed x13 -> x0, local copies, waits for them, and re-layouts: 5.18 us -> none
    pallas_call x0 -> x1, Pallas kernels: none -> 2.16 us  [per_device(): pl.pallas_call(store, out_shape=shapes, in_specs=[any_space] * 5, out_spe...]
where the time goes in v2:
time: 43.4 us; the launch traced here: 43.2 us
  Pallas kernels  42.6 us (98%)
  between operations  0.64 us (1%)
    pallas_call x1, Pallas kernels, per_device(): pl.pallas_call(functools.partial(kernel, (nz, ny, nh, blocks, heads), lim...  40.4 us
    pallas_call x1, Pallas kernels, per_device(): pl.pallas_call(store, out_shape=shapes, in_specs=[any_space] * 5, out_spe...  2.16 us

profile of v2, /device:TPU:1, one launch (start us, length us, event | category | flops | bytes accessed | tf_op | source)
XLA Modules:
  0.0 43.2 jit_solution(193152946860089108)
XLA Ops:
  0.6 40.4 %shard_map.146 = (bf16[1024,512]{1,0:T(8,128)(2,1)}, bf16[64,1024]{1,0:T(8,128)(2,1)}, bf16[64,1024]{1,0:T(8,128)(2,1)}, f32[64,64]{1,0:T(8,128)}, f32[1,8]{1,0:T(1,128)}) custom-call(bf16[1024,512]{1,0:T(8,128)(2,1)} %refs_0_.1, s32[16,1024]{1,0:T(8,128)} %bitcast.15, bf16[64,1024]{1,0:T(8,128)(2,1)} %bitcast.12, s32[2,1024]{1,0:T(2,128)} %bitcast.18, ...), custom_call_target="tpu_custom_call" | custom-call | tf_op jit(solution)/shard_map/pallas_call | solution.py:432
  41.1 2.2 %shard_map.147 = (bf16[1024,512]{1,0:T(8,128)(2,1)}, bf16[64,1024]{1,0:T(8,128)(2,1)}, bf16[64,1024]{1,0:T(8,128)(2,1)}, f32[64,64]{1,0:T(8,128)}, f32[1,8]{1,0:T(1,128)}) custom-call(bf16[1024,512]{1,0:T(8,128)(2,1)} %get-tuple-element.15.refs_0_, bf16[64,1024]{1,0:T(8,128)(2,1)} %get-tuple-element.16.refs_1_, bf16[64,1024]{1,0:T(8,128)(2,1)} %get-tuple-element.17.refs_2_, ...), custom_call_target="tpu_custom_call" | custom-call | tf_op jit(solution)/shard_map/pallas_call | solution.py:488

commit v3 on v2

--- a/solution.py
+++ b/solution.py
@@ -10,7 +10,7 @@
 
 WINDOW = 128
 LAGS = (4, 8, 12)
-SHARES = 4
+SHARES = 1
 HEAD = 64
 PAIR = 2 * HEAD
 clip_scale = 64.0
@@ -39,11 +39,11 @@
 def kernel(sizes, limit_value, *refs):
     (
         qe_hbm, qx_hbm, kt_hbm, kx_hbm, vt_hbm, vx_hbm, qc_hbm, kc_hbm, sinks, rot_hbm, do_hbm,
-        gq_hbm, gk_hbm, gv_hbm, gr_hbm, gs_hbm,
+        g_s, gk_s, gv_s, gr_s, gs_s,
         q_s, d_s, mq_s, qx_s, kt_s, kx_s, vt_s, vx_s, qc_s, kc_s, rot_s,
-        scale_s, kv_t, k_row, v_row, dk_s, dv_s, d2_s, w_s, rb_s, part_s, sinkacc, tri_s, back_in, back_in_v, g_s, gk_s, gv_s, gr_s, gs_s,
+        scale_s, kv_t, k_row, v_row, dk_s, dv_s, d2_s, w_s, rb_s, part_s, sinkacc, tri_s, back_in, back_in_v,
         buf_a1, buf_b1, buf_a2, buf_b2, sq_buf,
-        q_sem, d_sem, g_sem, in_sem, out_sem, halo_sem, back_sem,
+        q_sem, d_sem, in_sem, halo_sem, back_sem,
         a1_send, a1_recv, b1_send, b1_recv, a2_send, a2_recv, b2_send, b2_recv, h_send, h_recv,
     ) = refs
     nz, ny, nh, blocks, heads = sizes
@@ -85,10 +85,6 @@
         rows = pl.ds(pl.multiple_of(b * WINDOW, WINDOW), WINDOW)
         return pltpu.make_async_copy(do_hbm.at[rows], d_s.at[rows], d_sem.at[b])
 
-    def g_copy(b):
-        rows = pl.ds(pl.multiple_of(b * WINDOW, WINDOW), WINDOW)
-        return pltpu.make_async_copy(g_s.at[rows], gq_hbm.at[rows], g_sem.at[b])
-
     for n in range(blocks):
         b = [1, 2, 3, 4, 0, 5, 6, 7][n]
         q_copy(b).start()
@@ -126,7 +122,7 @@
         rows_of(cb)
         return carry
 
-    lax.fori_loop(1, blocks + 1, rows_step, 0)
+    lax.fori_loop(1, blocks + 1, rows_step, 0, unroll=True)
 
     for c in small_copies[4:]:
         c.wait()
@@ -163,6 +159,10 @@
         jnp.concatenate([jnp.full((1, WINDOW), sinks[2 * pr + h], f32) for h in range(2)], axis=1)
         for pr in range(pairs)
     ]
+
+    ahead = lax.rem(lax.broadcasted_iota(jnp.int32, (8, 2 * WINDOW), 1), WINDOW) - lax.broadcasted_iota(
+        jnp.int32, (8, 2 * WINDOW), 0
+    )
 
     def step(n, carry):
         @pl.when(n == 1)
@@ -184,10 +184,14 @@
             wide = pl.ds(pl.multiple_of(b * WINDOW, WINDOW), 2 * WINDOW)
             views.append((b, cols, wide))
         hidden = jnp.where((both[0] == 0) & (me_s == 0), negative, 0.0)
-        tri = p_iota <= i_iota
         trib = tri_s[...]
         units = [(k, pr) for k in range(2) for pr in range(pairs)]
         hold = {}
+
+        def choose(now, past):
+            return jnp.concatenate(
+                [jnp.where(ahead >= r, now[r : r + 8], past[r : r + 8]) for r in range(0, WINDOW, 8)], axis=0
+            )
 
         def stage_a(k, pr):
             b, cols, wide = views[k]
@@ -199,9 +203,9 @@
             d2_s[b, :, 2 * pr * WINDOW : 2 * (pr + 1) * WINDOW] = d2
             s_all = mm(k_row[wide, :], q2)
             before = s_all[:WINDOW] + hidden if k == 0 else s_all[:WINDOW]
-            s = jnp.where(tri, s_all[WINDOW:], before)
+            s = choose(s_all[WINDOW:], before)
             dp_all = mm(v_row[wide, :], d2)
-            dp = jnp.where(tri, dp_all[WINDOW:], dp_all[:WINDOW])
+            dp = choose(dp_all[WINDOW:], dp_all[:WINDOW])
             hold[k, pr] = (q2, s, dp)
 
         def stage_b(k, pr):
@@ -320,7 +324,6 @@
         for pr in range(pairs):
             lanes = slice(pr * PAIR, (pr + 1) * PAIR)
             g_s[cols, lanes] = mm(mq_s[lanes, cols].T, rb_s[...]).astype(bf16)
-        g_copy(b).start()
         return carry
 
     def values(b, carry):
@@ -362,52 +365,28 @@
     back_v.wait()
     dv_s[:, last] += back_in_v[...]
     gv_s[...] = dv_s[:, WINDOW:].astype(bf16)
-    outs = [
-        pltpu.make_async_copy(a, b, out_sem.at[n])
-        for n, (a, b) in enumerate([(gk_s, gk_hbm), (gv_s, gv_hbm), (gs_s, gs_hbm), (gr_s, gr_hbm)])
-    ]
-    for c in outs[:3]:
-        c.start()
     for c in copies_h:
         c.wait()
     norm = jnp.sqrt(total(sq_buf, nh)[:1, :HEAD])
     gr_s[...] = raw * (clip_scale / jnp.maximum(norm, limit_value))
-    outs[3].start()
-
-    def g_wait(b, carry):
-        g_copy(b).wait()
-        return carry
-
-    lax.fori_loop(0, blocks, g_wait, 0)
-    for c in outs:
-        c.wait()
 
 
 def store(*refs):
-    srcs, dsts, held, in_sems, out_sems = refs[:5], refs[5:10], refs[10:15], refs[15], refs[16]
-    parts = [(n, None) for n in (4, 3)]
+    srcs, dsts, sems = refs[:5], refs[5:10], refs[10]
     share = srcs[0].shape[0] // SHARES
-    parts += [(0, pl.ds(n * share, share)) for n in range(SHARES)]
-    parts += [(n, None) for n in (1, 2)]
+    parts = [(n, None) for n in (4, 3, 2, 1)] + [(0, pl.ds(n * share, share)) for n in range(SHARES)]
 
     def view(ref, rows):
         return ref if rows is None else ref.at[rows]
 
-    loads = [
-        pltpu.make_async_copy(view(srcs[n], rows), view(held[n], rows), in_sems.at[k])
+    copies = [
+        pltpu.make_async_copy(view(srcs[n], rows), view(dsts[n], rows), sems.at[k])
         for k, (n, rows) in enumerate(parts)
     ]
-    stores = [
-        pltpu.make_async_copy(view(held[n], rows), view(dsts[n], rows), out_sems.at[k])
-        for k, (n, rows) in enumerate(parts)
-    ]
-    for c in loads:
+    for c in copies:
         c.start()
-    for c, d in zip(loads, stores):
-        c.wait()
-        d.start()
-    for d in stores:
-        d.wait()
+    for c in copies:
+        c.wait()
 
 
 def per_device(split, ns, nh, qe, qx, ke, kx, ve, vx, qc, kc, sinks, rot, dout):
@@ -433,7 +412,7 @@
         functools.partial(kernel, (nz, ny, nh, blocks, heads), limit_value),
         out_shape=shapes,
         in_specs=[any_space] * 8 + [pl.BlockSpec(memory_space=pltpu.SMEM)] + [any_space] * 2,
-        out_specs=(any_space,) * 5,
+        out_specs=(pl.BlockSpec(memory_space=pltpu.VMEM),) * 5,
         scratch_shapes=[
             vmem((tokens, width), bf16),
             vmem((tokens, width), bf16),
@@ -460,11 +439,6 @@
             vmem((WINDOW, 2 * WINDOW), bf16),
             vmem((HEAD, WINDOW), f32),
             vmem((HEAD, WINDOW), f32),
-            vmem((tokens, width), bf16),
-            vmem((HEAD, tokens), bf16),
-            vmem((HEAD, tokens), bf16),
-            vmem((HEAD, HEAD), f32),
-            vmem((1, heads), f32),
             vmem((nz, cut, 128), bf16),
             vmem((ny, rest, 128), bf16),
             vmem((ny, cut, 128), bf16),
@@ -472,9 +446,7 @@
             vmem((nh, 8, 128), f32),
             dma((blocks,)),
             dma((blocks,)),
-            dma((blocks,)),
             dma((8,)),
-            dma((4,)),
             dma((2,)),
             dma((4,)),
             dma((nz,)), dma((nz,)), dma((ny,)), dma((ny,)),
@@ -482,15 +454,16 @@
             dma((nh,)), dma((nh,)),
         ],
         compiler_params=pltpu.CompilerParams(
-            collective_id=0, has_side_effects=True, vmem_limit_bytes=61 * 1024 * 1024
+            collective_id=0, has_side_effects=True, vmem_limit_bytes=52 * 1024 * 1024
         ),
-    )(qe, qx.T, ke.T, kx.T, ve.T, vx.T, qc.T, kc.T, sinks, rot.reshape(HEAD, HEAD), dout)
+    )(*[pltpu.with_memory_space_constraint(x, pltpu.HBM) for x in (qe, qx.T, ke.T, kx.T, ve.T, vx.T, qc.T, kc.T, sinks, rot.reshape(HEAD, HEAD), dout)])
     gq, gk, gv, gr, gs = pl.pallas_call(
         store,
         out_shape=shapes,
         in_specs=[any_space] * 5,
         out_specs=(any_space,) * 5,
-        scratch_shapes=[vmem(x.shape, x.dtype) for x in shapes] + [dma((SHARES + 4,))] * 2,
+        scratch_shapes=[dma((SHARES + 4,))],
+        compiler_params=pltpu.CompilerParams(vmem_limit_bytes=4 * 1024 * 1024),
     )(*outs)
     return (gq, gk.T, gv.T, gr[None], gs.reshape(heads))
 

time: 43.4 us -> 41.3 us (0.952)
  Pallas kernels: 42.6 us -> 40.5 us
    pallas_call x1, Pallas kernels: 40.4 us -> 39.4 us  [per_device(): pl.pallas_call(functools.partial(kernel, (nz, ny, nh, blocks, heads), lim...]
    pallas_call x1, Pallas kernels: 2.16 us -> 1.12 us  [per_device(): pl.pallas_call(store, out_shape=shapes, in_specs=[any_space] * 5, out_spe...]
where the time goes in v3:
time: 41.3 us; the launch traced here: 41.1 us
  Pallas kernels  40.5 us (98%)
  between operations  0.64 us (2%)
    pallas_call x1, Pallas kernels, per_device(): pl.pallas_call(functools.partial(kernel, (nz, ny, nh, blocks, heads), lim...  39.4 us
    pallas_call x1, Pallas kernels, per_device(): pl.pallas_call(store, out_shape=shapes, in_specs=[any_space] * 5, out_spe...  1.12 us

profile of v3, /device:TPU:1, one launch (start us, length us, event | category | flops | bytes accessed | tf_op | source)
XLA Modules:
  0.0 41.1 jit_solution(11661104283331763178)
XLA Ops:
  0.6 39.4 %shard_map.146 = (bf16[1024,512]{1,0:T(8,128)(2,1)S(1)}, bf16[64,1024]{1,0:T(8,128)(2,1)S(1)}, bf16[64,1024]{1,0:T(8,128)(2,1)S(1)}, f32[64,64]{1,0:T(8,128)S(1)}, f32[1,8]{1,0:T(1,128)S(1)}) custom-call(bf16[1024,512]{1,0:T(8,128)(2,1)} %refs_0_.1, s32[16,1024]{1,0:T(8,128)} %bitcast.15, bf16[64,1024]{1,0:T(8,128)(2,1)} %bitcast.12, s32[2,1024]{1,0:T(2,128)} %bitcast.18, ...), custom_call_target="tpu_custom_call" | custom-call | tf_op jit(solution)/shard_map/pallas_call | solution.py:411
  40.0 1.1 %shard_map.147 = (bf16[1024,512]{1,0:T(8,128)(2,1)}, bf16[64,1024]{1,0:T(8,128)(2,1)}, bf16[64,1024]{1,0:T(8,128)(2,1)}, f32[64,64]{1,0:T(8,128)}, f32[1,8]{1,0:T(1,128)}) custom-call(bf16[1024,512]{1,0:T(8,128)(2,1)S(1)} %get-tuple-element.15.refs_0_, bf16[64,1024]{1,0:T(8,128)(2,1)S(1)} %get-tuple-element.16.refs_1_, ...), custom_call_target="tpu_custom_call" | custom-call | tf_op jit(solution)/shard_map/pallas_call | solution.py:460

commit v4 on v3

--- a/solution.py
+++ b/solution.py
@@ -57,9 +57,15 @@
     def seq_dev(s):
         return (s, me_h)
 
-    z_peers = [(lax.rem(me_z + k, nz)) for k in range(1, nz)]
-    y_peers = [(lax.rem(me_y + k, ny)) for k in range(1, ny)]
-    h_peers = [(lax.rem(me_h + k, nh)) for k in range(1, nh)]
+    def far_first(n):
+        return sorted(range(1, n), key=lambda k: -min(k, n - k))
+
+    z_peers = [lax.rem(me_z + k, nz) for k in far_first(nz)]
+    y_peers = [lax.rem(me_y + k, ny) for k in far_first(ny)]
+    chips = nh // 2
+    me_x, me_c = me_h // 2, lax.rem(me_h, 2)
+    steps = [(k, other) for k in far_first(chips) + [0] for other in (1, 0) if k or other]
+    h_peers = [2 * lax.rem(me_x + k, chips) + (1 - me_c if other else me_c) for k, other in steps]
 
     barrier = pltpu.get_barrier_semaphore()
     targets = [(nxt, me_h), (prv, me_h)]
@@ -165,7 +171,7 @@
     )
 
     def step(n, carry):
-        @pl.when(n == 1)
+        @pl.when(n == 0)
         def _():
             pl.semaphore_wait(barrier, len(targets))
             halo.start()
@@ -266,21 +272,23 @@
         return carry
 
     lax.fori_loop(0, blocks // 2, step, 0)
+    last = pl.ds(blocks * WINDOW, WINDOW)
+
+    def key_part(first, count):
+        width = count * WINDOW
+        at, ext = slice(first * WINDOW, first * WINDOW + width), slice((first + 1) * WINDOW, (first + 1) * WINDOW + width)
+        words = jnp.concatenate([jnp.broadcast_to(kc_s[r : r + 1, at], (16, width)) for r in range(4)], axis=0)
+        flags = jnp.left_shift(1, lax.rem(lax.broadcasted_iota(jnp.int32, (HEAD, width), 0), 16))
+        mk = jnp.where(jnp.bitwise_and(words, flags) != 0, dk_s[:, ext] * temper, 0.0).astype(bf16)
+        gk_s[:, at] = mk
+        return mm(kv_t[:HEAD, ext], mk, NT) * (1.0 / temper)
+
+    part = part_s[...] + key_part(0, blocks - 1)
     back.wait()
-
-    last = pl.ds(blocks * WINDOW, WINDOW)
     dk_s[:, last] += back_in[...]
-
-    keep = jnp.bitwise_and(
-        jnp.concatenate([jnp.broadcast_to(kc_s[r : r + 1, :], (16, blocks * WINDOW)) for r in range(4)], axis=0),
-        jnp.left_shift(1, lax.rem(lax.broadcasted_iota(jnp.int32, (HEAD, blocks * WINDOW), 0), 16)),
-    ) != 0
-    mk = jnp.where(keep, dk_s[:, WINDOW:] * temper, 0.0).astype(bf16)
-    gk_s[...] = mk
-    part_s[...] += mm(kv_t[:HEAD, WINDOW:], mk, NT) * (1.0 / temper)
+    part = part + key_part(blocks - 1, 1)
 
     cut = buf_a1.shape[1]
-    part = part_s[...]
     folded = jnp.concatenate([part[: HEAD // 2], part[HEAD // 2 :]], axis=1)
     buf_a1[pl.ds(me_z, 1)] = folded[:cut].astype(bf16)[None]
     buf_b1[pl.ds(me_y, 1)] = (
@@ -316,8 +324,8 @@
             acc = acc + buf[k].astype(f32)
         return acc
 
-    copies_a = exchange(buf_a1, me_z, z_peers, along_z, a1_send, a1_recv)
-    copies_b = exchange(buf_b1, me_y, y_peers, along_y, b1_send, b1_recv)
+    copies_b = first_b = exchange(buf_b1, me_y, y_peers, along_y, b1_send, b1_recv)
+    copies_a = first_a = exchange(buf_a1, me_z, z_peers, along_z, a1_send, a1_recv)
 
     def turn(b, carry):
         cols = pl.ds(pl.multiple_of(b * WINDOW, WINDOW), WINDOW)
@@ -337,18 +345,18 @@
     back_v.start()
     lax.fori_loop(1, blocks, values, 0)
     for c in copies_a:
-        c.wait()
+        c.wait_recv()
     buf_a2[pl.ds(me_y, 1)] = total(buf_a1, nz).astype(bf16)[None]
     copies_a = exchange(buf_a2, me_y, y_peers, along_y, a2_send, a2_recv)
     for c in copies_b:
-        c.wait()
+        c.wait_recv()
     buf_b2[pl.ds(me_z, 1)] = total(buf_b1, ny).astype(bf16)[None]
     copies_b = exchange(buf_b2, me_z, z_peers, along_z, b2_send, b2_recv)
     lax.fori_loop(0, blocks, turn, 0)
     for c in copies_a:
-        c.wait()
+        c.wait_recv()
     for c in copies_b:
-        c.wait()
+        c.wait_recv()
     tot_a = total(buf_a2, ny)
     tot_b = total(buf_b2, nz)
     rows_b = HEAD // 2 - cut
@@ -358,15 +366,17 @@
         rot_s[...], summed, NN, precision=lax.Precision.HIGHEST, preferred_element_type=f32
     )
     sq = jnp.sum(jnp.sum(raw * raw, axis=0, keepdims=True), axis=1, keepdims=True)
-    sq_buf[pl.ds(me_h, 1)] = jnp.broadcast_to(sq, (8, 128))[None]
+    sq_buf[pl.ds(me_h, 1)] = jnp.broadcast_to(sq, (1, 128))[None]
     copies_h = exchange(sq_buf, me_h, h_peers, along_h, h_send, h_recv)
     gs_s[...] = jnp.sum(tot_b[rows_b : rows_b + heads].T, axis=0, keepdims=True)
     gk_s[...] = mm(rlow, gk_s[...]).astype(bf16)
     back_v.wait()
     dv_s[:, last] += back_in_v[...]
     gv_s[...] = dv_s[:, WINDOW:].astype(bf16)
+    for c in first_a + first_b + copies_a + copies_b + copies_h:
+        c.wait_send()
     for c in copies_h:
-        c.wait()
+        c.wait_recv()
     norm = jnp.sqrt(total(sq_buf, nh)[:1, :HEAD])
     gr_s[...] = raw * (clip_scale / jnp.maximum(norm, limit_value))
 
@@ -443,7 +453,7 @@
             vmem((ny, rest, 128), bf16),
             vmem((ny, cut, 128), bf16),
             vmem((nz, rest, 128), bf16),
-            vmem((nh, 8, 128), f32),
+            vmem((nh, 1, 128), f32),
             dma((blocks,)),
             dma((blocks,)),
             dma((8,)),

time: 41.3 us -> 40.7 us (0.985)
  Pallas kernels: 40.5 us -> 39.9 us
    pallas_call x1, Pallas kernels: 39.4 us -> 38.7 us  [per_device(): pl.pallas_call(functools.partial(kernel, (nz, ny, nh, blocks, heads), lim...]
where the time goes in v4:
time: 40.7 us; the launch traced here: 40.5 us
  Pallas kernels  39.9 us (98%)
  between operations  0.64 us (2%)
    pallas_call x1, Pallas kernels, per_device(): pl.pallas_call(functools.partial(kernel, (nz, ny, nh, blocks, heads), lim...  38.7 us
    pallas_call x1, Pallas kernels, per_device(): pl.pallas_call(store, out_shape=shapes, in_specs=[any_space] * 5, out_spe...  1.12 us

profile of v4, /device:TPU:1, one launch (start us, length us, event | category | flops | bytes accessed | tf_op | source)
XLA Modules:
  0.0 40.5 jit_solution(13872216058897604312)
XLA Ops:
  0.6 38.7 %shard_map.146 = (bf16[1024,512]{1,0:T(8,128)(2,1)S(1)}, bf16[64,1024]{1,0:T(8,128)(2,1)S(1)}, bf16[64,1024]{1,0:T(8,128)(2,1)S(1)}, f32[64,64]{1,0:T(8,128)S(1)}, f32[1,8]{1,0:T(1,128)S(1)}) custom-call(bf16[1024,512]{1,0:T(8,128)(2,1)} %refs_0_.1, s32[16,1024]{1,0:T(8,128)} %bitcast.15, bf16[64,1024]{1,0:T(8,128)(2,1)} %bitcast.12, s32[2,1024]{1,0:T(2,128)} %bitcast.18, ...), custom_call_target="tpu_custom_call" | custom-call | tf_op jit(solution)/shard_map/pallas_call | solution.py:421
  39.4 1.1 %shard_map.147 = (bf16[1024,512]{1,0:T(8,128)(2,1)}, bf16[64,1024]{1,0:T(8,128)(2,1)}, bf16[64,1024]{1,0:T(8,128)(2,1)}, f32[64,64]{1,0:T(8,128)}, f32[1,8]{1,0:T(1,128)}) custom-call(bf16[1024,512]{1,0:T(8,128)(2,1)S(1)} %get-tuple-element.15.refs_0_, bf16[64,1024]{1,0:T(8,128)(2,1)S(1)} %get-tuple-element.16.refs_1_, ...), custom_call_target="tpu_custom_call" | custom-call | tf_op jit(solution)/shard_map/pallas_call | solution.py:470

commit v5 on v4

--- a/solution.py
+++ b/solution.py
@@ -67,14 +67,6 @@
     steps = [(k, other) for k in far_first(chips) + [0] for other in (1, 0) if k or other]
     h_peers = [2 * lax.rem(me_x + k, chips) + (1 - me_c if other else me_c) for k, other in steps]
 
-    barrier = pltpu.get_barrier_semaphore()
-    targets = [(nxt, me_h), (prv, me_h)]
-    targets += [(z * ny + me_y, me_h) for z in z_peers]
-    targets += [(me_z * ny + y, me_h) for y in y_peers]
-    targets += [(me_s, h) for h in h_peers]
-    for dev in targets:
-        pl.semaphore_signal(barrier, inc=1, device_id=dev, device_id_type=MESH)
-
     small = [
         (kt_hbm, kt_s), (kx_hbm, kx_s), (vt_hbm, vt_s), (vx_hbm, vx_s),
         (qx_hbm, qx_s), (qc_hbm, qc_s), (kc_hbm, kc_s), (rot_hbm, rot_s),
@@ -82,6 +74,16 @@
     small_copies = [pltpu.make_async_copy(a, b, in_sem.at[n]) for n, (a, b) in enumerate(small)]
     for c in small_copies[:4]:
         c.start()
+
+    barrier = pltpu.get_barrier_semaphore()
+    targets = []
+    for k in range(max(nz, ny, nh) - 1):
+        targets += [(z * ny + me_y, me_h) for z in z_peers[k : k + 1]]
+        targets += [(me_z * ny + y, me_h) for y in y_peers[k : k + 1]]
+        targets += [(me_s, h) for h in h_peers[k : k + 1]]
+    targets += [(nxt, me_h), (prv, me_h)]
+    for dev in targets:
+        pl.semaphore_signal(barrier, inc=1, device_id=dev, device_id_type=MESH)
 
     def q_copy(b):
         rows = pl.ds(pl.multiple_of(b * WINDOW, WINDOW), WINDOW)

time: 40.7 us -> 40.6 us (level)
  no operation moved by 1% of the time
where the time goes in v5:
time: 40.6 us; the launch traced here: 40.4 us
  Pallas kernels  39.8 us (98%)
  between operations  0.64 us (2%)
    pallas_call x1, Pallas kernels, per_device(): pl.pallas_call(functools.partial(kernel, (nz, ny, nh, blocks, heads), lim...  38.7 us
    pallas_call x1, Pallas kernels, per_device(): pl.pallas_call(store, out_shape=shapes, in_specs=[any_space] * 5, out_spe...  1.12 us

profile of v5, /device:TPU:1, one launch (start us, length us, event | category | flops | bytes accessed | tf_op | source)
XLA Modules:
  0.0 40.4 jit_solution(11987652909613908277)
XLA Ops:
  0.6 38.7 %shard_map.146 = (bf16[1024,512]{1,0:T(8,128)(2,1)S(1)}, bf16[64,1024]{1,0:T(8,128)(2,1)S(1)}, bf16[64,1024]{1,0:T(8,128)(2,1)S(1)}, f32[64,64]{1,0:T(8,128)S(1)}, f32[1,8]{1,0:T(1,128)S(1)}) custom-call(bf16[1024,512]{1,0:T(8,128)(2,1)} %refs_0_.1, s32[16,1024]{1,0:T(8,128)} %bitcast.15, bf16[64,1024]{1,0:T(8,128)(2,1)} %bitcast.12, s32[2,1024]{1,0:T(2,128)} %bitcast.18, ...), custom_call_target="tpu_custom_call" | custom-call | tf_op jit(solution)/shard_map/pallas_call | solution.py:423
  39.3 1.1 %shard_map.147 = (bf16[1024,512]{1,0:T(8,128)(2,1)}, bf16[64,1024]{1,0:T(8,128)(2,1)}, bf16[64,1024]{1,0:T(8,128)(2,1)}, f32[64,64]{1,0:T(8,128)}, f32[1,8]{1,0:T(1,128)}) custom-call(bf16[1024,512]{1,0:T(8,128)(2,1)S(1)} %get-tuple-element.15.refs_0_, bf16[64,1024]{1,0:T(8,128)(2,1)S(1)} %get-tuple-element.16.refs_1_, ...), custom_call_target="tpu_custom_call" | custom-call | tf_op jit(solution)/shard_map/pallas_call | solution.py:472
